TPU v7x, 512 devices: a whole 4x8x8 slice. The times are simulated.
512 devices in a mesh: seq: 64 (over x, y, core), head: 8 (over z).
Axes of the slice: x: 4, y: 8, z: 8, core: 2. Of those that a mesh axis runs over, the one named last changes fastest.
Arguments:
- inner_x: bfloat16 [8192, 8192], P('seq', 'head'), may hold values from -6 to 6
- in_proj_b: bfloat16 [8192, 128], P('seq'), may hold values from -0.1796875 to 0.1796875
- in_proj_c: bfloat16 [8192, 128], P('seq'), may hold values from -0.1796875 to 0.1796875
- log_decay: float32 [128, 8192], P('head', 'seq'), may hold values from -1 to 0
- out_grad: bfloat16 [8192, 8192], P('seq', 'head'), may hold values from -6 to 6
Outputs:
- grad_inner_x: bfloat16 [8192, 8192], P('seq', 'head')
- grad_b: bfloat16 [8192, 128], P('seq')
- grad_c: bfloat16 [8192, 128], P('seq')
- grad_log_decay: float32 [128, 8192], P('head', 'seq')
All inputs are finite; a program needn't handle non-finite values.
Results may differ from a plain program's by a relative error of at most 0.0057.
Values may be sent and summed in bfloat16 or wider, within the bound.
No kernel may reach another device: no remote copies, remote signals or barrier semaphores. Data moves between devices by JAX's collectives and lax.ppermute only.
A program may use at most 192 MiB of HBM per device.

v0:
```python
import jax
import jax.numpy as jnp
from jax import lax
from jax.sharding import PartitionSpec as P


def carried_in(part, axis, combine, identity, reverse):
    count = lax.axis_size(axis)
    place = lax.axis_index(axis)
    ahead = count - 1 - place if reverse else place
    gathered = jax.tree.map(lambda a: lax.all_gather(a, axis), part)
    state = jax.tree.map(lambda a, e: jnp.zeros_like(a) + jnp.asarray(e, a.dtype), part, identity)

    def one(turn, state):
        source = count - 1 - turn if reverse else turn
        return combine(
            state, jax.tree.map(lambda a: lax.dynamic_index_in_dim(a, source, 0, False), gathered)
        )

    return lax.fori_loop(0, ahead, one, state)


def combine(earlier, later):
    return (earlier[0] + later[0], jnp.exp(later[0])[:, None, None] * earlier[1] + later[1])


def group_step(
    running, inputs, b_mat, b_float, c_float, scores, lower_mask, upper_table, lower_table
):
    mixed_sum, b_cross, c_cross = running
    inner_g, grad_g, cumulative, total, entry, adjoint = inputs
    gaps = jnp.where(lower_mask[None], cumulative[:, :, None] - cumulative[:, None, :], 0.0)
    decays = jnp.where(lower_mask[None], jnp.exp(gaps), 0.0)
    kernel = (decays * scores[None]).astype(jnp.bfloat16)
    to_end = jnp.exp(total[:, None] - cumulative)
    from_start = jnp.exp(cumulative)
    adjoint_b = adjoint.astype(jnp.bfloat16)
    state_b = entry.astype(jnp.bfloat16)
    x_adjoint = jnp.einsum("gtp,gpn->gtn", inner_g, adjoint_b, preferred_element_type=jnp.float32)
    grad_state = jnp.einsum("gtp,gpn->gtn", grad_g, state_b, preferred_element_type=jnp.float32)
    b_adjoint = jnp.einsum("tn,gpn->gtp", b_mat, adjoint_b, preferred_element_type=jnp.float32)
    intra_grad = jnp.einsum("gus,gup->gsp", kernel, grad_g, preferred_element_type=jnp.float32)
    grad_x = intra_grad + to_end[:, :, None] * b_adjoint
    pairs = jnp.einsum("gup,gsp->gus", grad_g, inner_g, preferred_element_type=jnp.float32)
    mixed = decays * pairs
    weighted = mixed * scores[None]
    colsum = jnp.sum(weighted, axis=1)
    rowsum = jnp.sum(weighted, axis=2)
    increments = colsum - jnp.concatenate(
        [jnp.zeros((rowsum.shape[0], 1), jnp.float32), rowsum[:, :-1]], axis=1
    )
    inner_q = jnp.dot(increments, upper_table, precision=lax.Precision.HIGHEST)
    alphas = from_start * jnp.sum(grad_state * c_float[None], axis=2)
    suffix = jnp.dot(alphas, lower_table, precision=lax.Precision.HIGHEST)
    betas = to_end * jnp.sum(x_adjoint * b_float[None], axis=2)
    prefix = jnp.dot(betas, upper_table, precision=lax.Precision.HIGHEST)
    constant = jnp.exp(total) * jnp.sum(adjoint * entry, axis=(1, 2))
    decay_grad = (
        inner_q
        + suffix
        + prefix
        + constant[:, None]
        - jnp.sum(grad_x * inner_g.astype(jnp.float32), axis=2)
    )
    b_more = jnp.einsum("gt,gtn->tn", to_end, x_adjoint, precision=lax.Precision.HIGHEST)
    c_more = jnp.einsum("gt,gtn->tn", from_start, grad_state, precision=lax.Precision.HIGHEST)
    updated = (mixed_sum + jnp.sum(mixed, axis=0), b_cross + b_more, c_cross + c_more)
    return (updated, (grad_x.astype(jnp.bfloat16), decay_grad))


def per_device(inner_x, in_proj_b, in_proj_c, log_decay, out_grad):
    tokens = inner_x.shape[0]
    head_count = log_decay.shape[0]
    head_width = inner_x.shape[1] // head_count
    state_width = in_proj_b.shape[1]
    inner_heads = inner_x.reshape(tokens, head_count, head_width).transpose(1, 0, 2)
    grad_heads = out_grad.reshape(tokens, head_count, head_width).transpose(1, 0, 2)
    cumulative = jnp.cumsum(log_decay, axis=1)
    totals = cumulative[:, -1]
    weighted_x = (
        inner_heads.astype(jnp.float32) * jnp.exp(totals[:, None] - cumulative)[:, :, None]
    ).astype(jnp.bfloat16)
    weighted_grad = (grad_heads.astype(jnp.float32) * jnp.exp(cumulative)[:, :, None]).astype(
        jnp.bfloat16
    )
    end_states = lax.dot_general(
        weighted_x, in_proj_b, (((1,), (0,)), ((), ())), preferred_element_type=jnp.float32
    )
    open_adjoints = lax.dot_general(
        weighted_grad, in_proj_c, (((1,), (0,)), ((), ())), preferred_element_type=jnp.float32
    )
    identity = (jnp.zeros_like(totals), jnp.zeros_like(end_states))
    entry_totals, entries = carried_in((totals, end_states), "seq", combine, identity, False)
    later_totals, adjoints = carried_in((totals, open_adjoints), "seq", combine, identity, True)
    scores = lax.dot_general(
        in_proj_c, in_proj_b, (((1,), (1,)), ((), ())), preferred_element_type=jnp.float32
    )
    rows = lax.broadcasted_iota(jnp.int32, (tokens, tokens), 0)
    cols = lax.broadcasted_iota(jnp.int32, (tokens, tokens), 1)
    lower_mask = rows >= cols
    upper_table = (rows <= cols).astype(jnp.float32)
    lower_table = lower_mask.astype(jnp.float32)
    b_float = in_proj_b.astype(jnp.float32)
    c_float = in_proj_c.astype(jnp.float32)
    group_size = 1
    while (
        group_size * 2 <= head_count
        and head_count % (group_size * 2) == 0
        and (group_size * 2 * tokens * tokens <= 1048576)
    ):
        group_size = group_size * 2
    group_count = head_count // group_size

    def grouped(array):
        return array.reshape((group_count, group_size) + array.shape[1:])

    start = (
        jnp.zeros((tokens, tokens), jnp.float32),
        jnp.zeros((tokens, state_width), jnp.float32),
        jnp.zeros((tokens, state_width), jnp.float32),
    )

    def scan_group(running, inputs):
        return group_step(
            running,
            inputs,
            in_proj_b,
            b_float,
            c_float,
            scores,
            lower_mask,
            upper_table,
            lower_table,
        )

    sums, outs = lax.scan(
        scan_group,
        start,
        (
            grouped(inner_heads),
            grouped(grad_heads),
            grouped(cumulative),
            grouped(totals),
            grouped(entries),
            grouped(adjoints),
        ),
    )
    mixed_sum, b_cross, c_cross = sums
    b_part = (
        lax.dot_general(
            mixed_sum, c_float, (((0,), (0,)), ((), ())), precision=lax.Precision.HIGHEST
        )
        + b_cross
    )
    c_part = jnp.dot(mixed_sum, b_float, precision=lax.Precision.HIGHEST) + c_cross
    b_sum, c_sum = lax.psum((b_part, c_part), "head")
    grad_b = b_sum.astype(jnp.bfloat16)
    grad_c = c_sum.astype(jnp.bfloat16)
    grad_heads_x = outs[0].reshape(head_count, tokens, head_width)
    grad_inner_x = grad_heads_x.transpose(1, 0, 2).reshape(tokens, head_count * head_width)
    decay_grads = outs[1].reshape(head_count, tokens)
    return (grad_inner_x, grad_b, grad_c, decay_grads)


def solution(mesh):
    in_specs = (
        P("seq", "head"),
        P("seq", None),
        P("seq", None),
        P("head", "seq"),
        P("seq", "head"),
    )
    out_specs = (P("seq", "head"), P("seq", None), P("seq", None), P("head", "seq"))
    return jax.shard_map(
        per_device, mesh=mesh, in_specs=in_specs, out_specs=out_specs, check_vma=False
    )
```

profile of v0, /device:TPU:62, one launch (start us, length us, event | category | flops | bytes accessed | tf_op | source)
XLA Modules:
  0.0 435.4 jit_solution(7235106244912824527)
XLA Ops:
  10.1 1.8 fusion.16
  13.1 1.8 fusion.17
  14.9 1.5 copy.23
  16.4 1.5 copy.24
  17.9 1.3 dynamic-slice.7
  20.1 125.3 %all-reduce.1 = f32[1024]{0:T(1024)S(1)} all-reduce(f32[1024]{0:T(1024)S(1)} %dynamic-update-slice), channel_id=2, replica_groups=mesh['seq'=64,'head'=8] {'seq'}, use_global_device_ids=true, to_apply=%add.1 | all-reduce | flops 1024 | bytes 8192
  148.6 12.0 %all-gather.6.cloned.1.call-done = f32[1024,64,128]{2,1,0:T(8,128)} async-done(((f32[16,64,128]{2,1,0:T(8,128)}), f32[1024,64,128]{2,1,0:T(8,128)}) %all-gather.6.cloned.1.call-update) | async-done | bytes 33554448 | tf_op jit(solution)/shard_map/all_gather | solution.py:11
  160.6 1.2 while.16
  160.6 1.2 bitcast_add_fusion.5
  161.8 1.7 fusion.10
  165.2 143.5 %all-gather.8.cloned.1.call-done = f32[1024,64,128]{2,1,0:T(8,128)} async-done(((f32[16,64,128]{2,1,0:T(8,128)}), f32[1024,64,128]{2,1,0:T(8,128)}) %all-gather.8.cloned.1.call-update) | async-done | bytes 33554448 | tf_op jit(solution)/shard_map/all_gather | solution.py:11
  308.8 76.9 %while.17 = (s32[]{:T(128)}, f32[16,64,128]{2,1,0:T(8,128)S(1)}, s32[]{:T(128)}, f32[64,16]{1,0:T(8,128)S(1)}, f32[64,16,64,128]{3,2,1,0:T(8,128)}, /*index=5*/s32[]{:T(128)}, s32[]{:T(128)}, s32[]{:T(128)}) while((s32[]{:T(128)}, f32[16,64,128]{2,1,0:T(8,128)S(1)}, s32[]{:T(128)}, f32[64,16]{1,0:T(8,128)S(1)}, f32[64,16,64,128]{3,2,1,0:T(8,128)}, ...), condition=%wide.region_6.7_spmd, body=%wide.region_5.6_spmd.sunk | while | flops 262149 | bytes 1573183 | solution.py:20
  308.9 1.2 bitcast_add_fusion.6
  310.1 1.2 bitcast_add_fusion.6
  311.3 1.2 bitcast_add_fusion.6
  312.6 1.2 bitcast_add_fusion.6
  313.8 1.2 bitcast_add_fusion.6
  315.1 1.2 bitcast_add_fusion.6
  316.3 1.2 bitcast_add_fusion.6
  317.6 1.2 bitcast_add_fusion.6
  318.8 1.2 bitcast_add_fusion.6
  320.0 1.2 bitcast_add_fusion.6
  321.3 1.2 bitcast_add_fusion.6
  322.5 1.2 bitcast_add_fusion.6
  323.8 1.2 bitcast_add_fusion.6
  325.0 1.2 bitcast_add_fusion.6
  326.2 1.2 bitcast_add_fusion.6
  327.5 1.2 bitcast_add_fusion.6
  328.7 1.2 bitcast_add_fusion.6
  330.0 1.2 bitcast_add_fusion.6
  331.2 1.2 bitcast_add_fusion.6
  332.4 1.2 bitcast_add_fusion.6
  333.7 1.2 bitcast_add_fusion.6
  334.9 1.2 bitcast_add_fusion.6
  336.2 1.2 bitcast_add_fusion.6
  337.4 1.2 bitcast_add_fusion.6
  338.6 1.2 bitcast_add_fusion.6
  339.9 1.2 bitcast_add_fusion.6
  341.1 1.2 bitcast_add_fusion.6
  342.4 1.2 bitcast_add_fusion.6
  343.6 1.2 bitcast_add_fusion.6
  344.8 1.2 bitcast_add_fusion.6
  346.1 1.2 bitcast_add_fusion.6
  347.3 1.2 bitcast_add_fusion.6
  348.6 1.2 bitcast_add_fusion.6
  349.8 1.2 bitcast_add_fusion.6
  351.0 1.2 bitcast_add_fusion.6
  352.3 1.2 bitcast_add_fusion.6
  353.5 1.2 bitcast_add_fusion.6
  354.8 1.2 bitcast_add_fusion.6
  356.0 1.2 bitcast_add_fusion.6
  358.5 1.2 bitcast_add_fusion.6
  359.7 1.2 bitcast_add_fusion.6
  362.2 1.2 bitcast_add_fusion.6
  363.5 1.2 bitcast_add_fusion.6
  367.2 1.2 bitcast_add_fusion.6
  370.9 1.2 bitcast_add_fusion.6
  374.6 1.2 bitcast_add_fusion.6
  378.3 1.2 bitcast_add_fusion.6
  382.1 1.2 bitcast_add_fusion.6
  383.3 1.2 bitcast_add_fusion.6
  389.9 1.8 copy.26
  394.5 32.7 %all-reduce.4 = (bf16[128,128]{1,0:T(8,128)(2,1)}, bf16[128,128]{1,0:T(8,128)(2,1)}) all-reduce(f32[128,128]{1,0:T(8,128)S(1)} %convolution_add_fusion.1, f32[128,128]{1,0:T(8,128)S(1)} %convolution_add_fusion), channel_id=1, replica_groups=mesh['seq'=64,'head'=8] {'head'}, use_global_device_ids=true, to_apply=%region_4.5 | all-reduce | flops 32768 | bytes 196608 | tf_op jit(solution)/shard_map/psum | solution.py:156
  427.1 1.5 fusion.1
  (112 shorter events, 32.6 us)
Async XLA Ops:
  7.2 382.2 %copy-start.1 = (bf16[128,128]{1,0:T(8,128)(2,1)S(1)}, bf16[128,128]{1,0:T(8,128)(2,1)}, u32[]{:S(2)}) copy-start(bf16[128,128]{1,0:T(8,128)(2,1)} %param.11) | copy-start | bytes 98308
  7.2 382.6 %copy-start = (bf16[128,128]{1,0:T(8,128)(2,1)S(1)}, bf16[128,128]{1,0:T(8,128)(2,1)}, u32[]{:S(2)}) copy-start(bf16[128,128]{1,0:T(8,128)(2,1)} %param.10) | copy-start | bytes 98308
  7.2 153.3 %all-gather.6.cloned.1.call-start = ((), (), s32[]{:S(2)}) async-start(), calls=%async_computation | async-start | bytes 34078720 | tf_op jit(solution)/shard_map/all_gather | solution.py:11
  12.0 296.8 %all-gather.8.cloned.1.call-start = ((), (), s32[]{:S(2)}) async-start(), calls=%async_computation.1 | async-start | bytes 34078720 | tf_op jit(solution)/shard_map/all_gather | solution.py:11
Sparse Core Ops, SparseCore 0:
  12.1 148.4 all-gather.5
  163.9 144.8 all-gather.7
where the time goes:
time: 439 us; the launch traced here: 435 us
  blocking collectives  158 us (36%)
  waiting for transfers between devices  156 us (36%)
  other arithmetic  79.9 us (18%)
  between operations  14.8 us (3%)
  matrix products  13.2 us (3%)
  local copies, waits for them, and re-layouts  11.5 us (3%)
    all_gather x2, waiting for transfers between devices, carried_in(): gathered = jax.tree.map(lambda a: lax.all_gather(a, axis), part)  155 us
    unnamed x1, blocking collectives  125 us
    add x63, other arithmetic, combine(): jnp.exp(later[0])[:, None, None] * earlier[1] + later[1]  74.8 us
    psum x1, blocking collectives, per_device(): b_sum, c_sum = lax.psum((b_part, c_part), 'head')  32.7 us
  transfers between devices with their start and end apart: 2, of which 2 were waited for; matrix products, arithmetic and copies ran while one was open for 3% of the time, Pallas kernels for 0%

commit v1 on v0

v1 whole, which is shorter than its diff:
```python
import functools

import jax
import jax.numpy as jnp
from jax import lax
from jax.experimental import pallas as pl
from jax.experimental.pallas import tpu as pltpu
from jax.sharding import PartitionSpec as P

F32 = jnp.float32
BF16 = jnp.bfloat16
HIGHEST = lax.Precision.HIGHEST
TOK = 128
LANES = 128
HALF = 64
HEADS = 16
PAIRS = 8
ROWS = 16
SEND_ROWS = 40


def nn(a, b, precision=None):
    return lax.dot_general(
        a, b, (((1,), (0,)), ((), ())), precision=precision, preferred_element_type=F32
    )


def nt(a, b, precision=None):
    return lax.dot_general(
        a, b, (((1,), (1,)), ((), ())), precision=precision, preferred_element_type=F32
    )


def iota(dim, shape=(TOK, LANES)):
    return lax.broadcasted_iota(jnp.int32, shape, dim)


def pair(g):
    return slice(g * LANES, (g + 1) * LANES)


def transposed(matrix):
    return matrix.astype(F32).T.astype(BF16)


def cumulative_columns(log_decay):
    lower = (iota(0) >= iota(1)).astype(F32)
    return nt(lower, log_decay, HIGHEST)


def spread(columns, g):
    rows = columns.shape[0]
    left = iota(1, (rows, LANES)) < HALF
    a = jnp.broadcast_to(columns[:, 2 * g : 2 * g + 1], (rows, LANES))
    b = jnp.broadcast_to(columns[:, 2 * g + 1 : 2 * g + 2], (rows, LANES))
    return jnp.where(left, a, b)


def states_kernel(x_ref, b_ref, c_ref, log_ref, grad_ref, send_ref, wx_ref, wg_ref):
    cum = cumulative_columns(log_ref[...])
    total = cum[TOK - 1 : TOK, :]
    to_end = jnp.exp(total - cum)
    from_start = jnp.exp(cum)
    b_t = transposed(b_ref[...])
    c_t = transposed(c_ref[...])
    for g in range(PAIRS):
        spread_start = spread(from_start, g)
        wx = (x_ref[:, pair(g)].astype(F32) * spread(to_end, g)).astype(BF16)
        wg = (grad_ref[:, pair(g)].astype(F32) * spread_start).astype(BF16)
        wx_ref[:, pair(g)] = wx
        wg_ref[:, pair(g)] = wg
        ends = nn(b_t, wx).astype(BF16)
        opens = nn(c_t, wg).astype(BF16)
        factor = jnp.broadcast_to(spread_start[TOK - 1 : TOK, :], (8, LANES))
        high = factor.astype(BF16).astype(F32)
        first = iota(0, (8, LANES)) == 0
        factors = jnp.where(first, high, factor - high).astype(BF16)
        for r in range(PAIRS):
            rows = slice(r * ROWS, (r + 1) * ROWS)
            send_ref[g * PAIRS + r] = jnp.concatenate([ends[rows], opens[rows], factors], axis=0)


def recurrence_kernel(got_ref, back_ref):
    count = got_ref.shape[0]

    def factor(k):
        parts = got_ref[k, 2 * ROWS : SEND_ROWS, :].astype(F32)
        return parts[0:1, :] + parts[1:2, :]

    entry = jnp.zeros((ROWS, LANES), F32)
    adjoint = jnp.zeros((ROWS, LANES), F32)
    for k in range(count):
        back_ref[k, 0:ROWS, :] = entry.astype(BF16)
        entry = factor(k) * entry + got_ref[k, 0:ROWS, :].astype(F32)
        m = count - 1 - k
        back_ref[m, ROWS : 2 * ROWS, :] = adjoint.astype(BF16)
        adjoint = factor(m) * adjoint + got_ref[m, ROWS : 2 * ROWS, :].astype(F32)


def intra_kernel(x_ref, b_ref, c_ref, log_ref, grad_ref, gx_ref, decay_ref, bc_ref):
    log_decay = log_ref[...]
    upper = (iota(0) <= iota(1)).astype(F32)
    cum_rows = nn(log_decay, upper, HIGHEST)
    cum = cumulative_columns(log_decay)
    b_mat = b_ref[...]
    c_mat = c_ref[...]
    scores = nt(b_mat, c_mat)
    later = iota(1) >= iota(0)
    before = iota(0) < iota(1)
    ends_after = (iota(0) >= iota(1)).astype(BF16)
    left = iota(1) < HALF
    mixed_sum = jnp.zeros((TOK, TOK), F32)
    for g in range(PAIRS):
        x_g = x_ref[:, pair(g)]
        grad_g = grad_ref[:, pair(g)]
        grad_x = jnp.zeros((TOK, LANES), F32)
        for j in range(2):
            h = 2 * g + j
            mine = left if j == 0 else jnp.logical_not(left)
            x_h = jnp.where(mine, x_g, jnp.zeros_like(x_g))
            grad_h = jnp.where(mine, grad_g, jnp.zeros_like(grad_g))
            pairs = nt(x_h, grad_g)
            gaps = cum_rows[h : h + 1, :] - cum[:, h : h + 1]
            decays = jnp.exp(jnp.where(later, gaps, -1e4))
            kernel = decays * scores
            mixed_sum = mixed_sum + decays * pairs
            grad_x = grad_x + nn(kernel.astype(BF16), grad_h)
            weighted = (kernel * pairs).astype(BF16)
            reach = nn(weighted, ends_after)
            decay_ref[h : h + 1, :] = jnp.sum(
                jnp.where(before, reach, 0.0), axis=0, keepdims=True
            )
        gx_ref[:, pair(g)] = grad_x
    high = mixed_sum.astype(BF16)
    low = (mixed_sum - high.astype(F32)).astype(BF16)
    mixed_t = mixed_sum.T
    high_t = mixed_t.astype(BF16)
    low_t = (mixed_t - high_t.astype(F32)).astype(BF16)
    bc_ref[0:TOK, :] = nn(high, c_mat) + nn(low, c_mat)
    bc_ref[TOK : 2 * TOK, :] = nn(high_t, b_mat) + nn(low_t, b_mat)


def cross_kernel(
    back_ref, x_ref, b_ref, c_ref, log_ref, grad_ref, wx_ref, wg_ref, gx_ref, inner_ref, bc_ref,
    out_ref, decay_ref, send_ref,
):
    cum = cumulative_columns(log_ref[...])
    total = cum[TOK - 1 : TOK, :]
    to_end = jnp.exp(total - cum)
    from_start = jnp.exp(cum)
    b_mat = b_ref[...]
    c_mat = c_ref[...]
    b_sum = bc_ref[0:TOK, :]
    c_sum = bc_ref[TOK : 2 * TOK, :]
    last = iota(0) == TOK - 1
    alphas = jnp.zeros((HEADS, TOK), F32)
    betas = jnp.zeros((HEADS, TOK), F32)
    for g in range(PAIRS):
        entry = back_ref[g * PAIRS : (g + 1) * PAIRS, 0:ROWS, :].reshape(TOK, LANES)
        adjoint = back_ref[g * PAIRS : (g + 1) * PAIRS, ROWS : 2 * ROWS, :].reshape(TOK, LANES)
        start_g = spread(from_start, g)
        cross = spread(to_end, g) * nn(b_mat, adjoint)
        out_ref[:, pair(g)] = (gx_ref[:, pair(g)] + cross).astype(BF16)
        beta = x_ref[:, pair(g)].astype(F32) * cross
        alpha = grad_ref[:, pair(g)].astype(F32) * (start_g * nn(c_mat, entry))
        overlap = jnp.sum(entry.astype(F32) * adjoint.astype(F32), axis=0, keepdims=True)
        alpha = alpha + jnp.where(last, start_g * overlap, 0.0)
        head_of = 2 * g + iota(1, (HEADS, LANES)) // HALF
        pick = (iota(0, (HEADS, LANES)) == head_of).astype(BF16)
        beta_high = beta.astype(BF16)
        alpha_high = alpha.astype(BF16)
        betas = betas + nt(pick, beta_high) + nt(pick, (beta - beta_high.astype(F32)).astype(BF16))
        alphas = (
            alphas + nt(pick, alpha_high) + nt(pick, (alpha - alpha_high.astype(F32)).astype(BF16))
        )
        b_sum = b_sum + nt(wx_ref[:, pair(g)], adjoint)
        c_sum = c_sum + nt(wg_ref[:, pair(g)], entry)
    before = (iota(0) < iota(1)).astype(F32)
    after = (iota(0) >= iota(1)).astype(F32)
    decay_ref[...] = inner_ref[...] + nn(betas, before, HIGHEST) + nn(alphas, after, HIGHEST)
    b_out = b_sum.astype(BF16)
    c_out = c_sum.astype(BF16)
    for z in range(send_ref.shape[0]):
        send_ref[z, 0:TOK, :] = b_out
        send_ref[z, TOK : 2 * TOK, :] = c_out


def call(body, outs, flops, *args):
    return pl.pallas_call(
        body,
        out_shape=[jax.ShapeDtypeStruct(s, d) for s, d in outs],
        compiler_params=pltpu.CompilerParams(vmem_limit_bytes=32 * 1024 * 1024),
        cost_estimate=pl.CostEstimate(flops=flops, bytes_accessed=2 << 20, transcendentals=0),
    )(*args)


def per_device(seq, heads, x, b_mat, c_mat, log_decay, grad):
    wide = (TOK, HEADS * HALF)
    send, wx, wg = call(
        states_kernel,
        [((seq, SEND_ROWS, LANES), BF16), (wide, BF16), (wide, BF16)],
        1 << 27,
        x, b_mat, c_mat, log_decay, grad,
    )
    got = lax.all_to_all(send, "seq", 0, 0, tiled=True)
    gx, inner, bc = call(
        intra_kernel,
        [(wide, F32), ((HEADS, TOK), F32), ((2 * TOK, LANES), F32)],
        1 << 29,
        x, b_mat, c_mat, log_decay, grad,
    )
    (back,) = call(recurrence_kernel, [((seq, 2 * ROWS, LANES), BF16)], 1 << 20, got)
    back = lax.all_to_all(back, "seq", 0, 0, tiled=True)
    grad_x, decay_grad, parts = call(
        cross_kernel,
        [(wide, BF16), ((HEADS, TOK), F32), ((heads, 2 * TOK, LANES), BF16)],
        1 << 28,
        back, x, b_mat, c_mat, log_decay, grad, wx, wg, gx, inner, bc,
    )
    parts = lax.all_to_all(parts, "head", 0, 0, tiled=True)
    sums = jnp.sum(parts.astype(F32), axis=0).astype(BF16)
    return grad_x, sums[:TOK], sums[TOK:], decay_grad


def solution(mesh):
    in_specs = (
        P("seq", "head"),
        P("seq", None),
        P("seq", None),
        P("head", "seq"),
        P("seq", "head"),
    )
    out_specs = (P("seq", "head"), P("seq", None), P("seq", None), P("head", "seq"))
    return jax.shard_map(
        functools.partial(per_device, mesh.shape["seq"], mesh.shape["head"]),
        mesh=mesh,
        in_specs=in_specs,
        out_specs=out_specs,
        check_vma=False,
    )
```

time: 439 us -> 93.5 us (0.21)
  the two profiles are of different devices: /device:TPU:62 before, /device:TPU:1 now
where the time goes in v1:
time: 93.5 us; the launch traced here: 93 us
  blocking collectives  58.7 us (63%)
  waiting for transfers between devices  15.3 us (16%)
  Pallas kernels  7.05 us (8%)
  starting transfers between devices  6.4 us (7%)
  local copies, waits for them, and re-layouts  4.76 us (5%)
    all_to_all x1, blocking collectives, per_device(): got = lax.all_to_all(send, 'seq', 0, 0, tiled=True)  31.6 us
    all_to_all x1, blocking collectives, per_device(): parts = lax.all_to_all(parts, 'head', 0, 0, tiled=True)  27.1 us
    all_to_all x1, waiting for transfers between devices, per_device(): back = lax.all_to_all(back, 'seq', 0, 0, tiled=True)  15.3 us
    pallas_call x4, Pallas kernels, call(): pl.pallas_call(body, out_shape=[jax.ShapeDtypeStruct(s, d) for s, d in ou...  7.05 us
    all_to_all x1, starting transfers between devices, per_device(): back = lax.all_to_all(back, 'seq', 0, 0, tiled=True)  6.4 us
    unnamed x20, local copies, waits for them, and re-layouts  4.13 us
  transfers between devices with their start and end apart: 1, of which 1 were waited for; matrix products, arithmetic and copies ran while one was open for 0% of the time, Pallas kernels for 2%

profile of v1, /device:TPU:1, one launch (start us, length us, event | category | flops | bytes accessed | tf_op | source)
XLA Modules:
  0.0 93.0 jit_solution(13413878029295821637)
XLA Ops:
  0.6 0.0 copy-start
  0.6 0.9 %copy-done = bf16[128,1024]{1,0:T(8,128)(2,1)S(1)} copy-done((bf16[128,1024]{1,0:T(8,128)(2,1)S(1)}, bf16[128,1024]{1,0:T(8,128)(2,1)}, u32[]{:S(2)}) %copy-start) | copy-done | bytes 262168
  1.6 0.0 copy-start.2
  1.6 0.9 %copy-done.2 = bf16[128,1024]{1,0:T(8,128)(2,1)S(1)} copy-done((bf16[128,1024]{1,0:T(8,128)(2,1)S(1)}, bf16[128,1024]{1,0:T(8,128)(2,1)}, u32[]{:S(2)}) %copy-start.2) | copy-done | bytes 262168
  2.5 0.0 copy-start.4
  2.5 0.8 copy-done.4
  3.3 0.0 copy-start.6
  3.3 0.8 copy-done.6
  4.1 0.0 copy-start.8
  4.1 0.7 copy-done.8
  4.7 1.1 %shard_map.84 = (bf16[64,40,128]{2,1,0:T(8,128)(2,1)S(1)}, bf16[128,1024]{1,0:T(8,128)(2,1)S(1)}, bf16[128,1024]{1,0:T(8,128)(2,1)S(1)}) custom-call(bf16[128,1024]{1,0:T(8,128)(2,1)S(1)} %copy-done, bf16[128,128]{1,0:T(8,128)(2,1)S(1)} %copy-done.4, bf16[128,128]{1,0:T(8,128)(2,1)S(1)} %copy-done.6, f32[16,128]{1,0:T(8,128)S(1)} %copy-done.8, ...), custom_call_target="tpu_custom_call" | custom-call | flops 134217728 | bytes 2097152 | tf_op jit(solution)/shard_map/pallas_call | solution.py:189
  5.9 31.6 %all_to_all.15.got_ref = bf16[64,40,128]{2,1,0:T(8,128)(2,1)S(1)} all-to-all(bf16[64,40,128]{2,1,0:T(8,128)(2,1)S(1)} %get-tuple-element.13), channel_id=1, replica_groups=mesh['seq'=64,'head'=8] {'seq'}, dimensions={0} | all-to-all | bytes 1310720 | tf_op jit(solution)/shard_map/all_to_all | solution.py:205
  37.4 1.0 %shard_map.85 = bf16[64,32,128]{2,1,0:T(8,128)(2,1)} custom-call(bf16[64,40,128]{2,1,0:T(8,128)(2,1)S(1)} %all_to_all.15.got_ref), custom_call_target="tpu_custom_call" | custom-call | flops 1048576 | bytes 2097152 | tf_op jit(solution)/shard_map/pallas_call | solution.py:189
  38.4 0.0 copy-start.1
  38.4 0.0 copy-start.3
  38.4 0.0 copy-start.5
  38.4 0.0 copy-start.7
  38.4 0.0 copy-start.9
  38.4 6.4 %all-to-all-start.1 = ((bf16[64,32,128]{2,1,0:T(8,128)(2,1)}), bf16[64,32,128]{2,1,0:T(8,128)(2,1)S(1)}, u32[]{:S(2)}, u32[]{:S(2)}) async-start(bf16[64,32,128]{2,1,0:T(8,128)(2,1)} %shard_map.85), calls=%async_computation.1 | async-start | bytes 1048576 | tf_op jit(solution)/shard_map/all_to_all | solution.py:213
  44.8 0.0 copy-done.1
  44.8 0.0 copy-done.3
  44.9 0.0 copy-done.5
  44.9 0.0 copy-done.7
  44.9 0.0 copy-done.9
  44.9 2.0 %shard_map.86 = (f32[128,1024]{1,0:T(8,128)S(1)}, f32[16,128]{1,0:T(8,128)S(1)}, f32[256,128]{1,0:T(8,128)S(1)}) custom-call(bf16[128,1024]{1,0:T(8,128)(2,1)S(1)} %copy-done.1, bf16[128,128]{1,0:T(8,128)(2,1)S(1)} %copy-done.5, bf16[128,128]{1,0:T(8,128)(2,1)S(1)} %copy-done.7, f32[16,128]{1,0:T(8,128)S(1)} %copy-done.9, bf16[128,1024]{1,0:T(8,128)(2,1)S(1)} %copy-done.3), custom_call_target="tpu_custom_call" | custom-call | flops 536870912 | bytes 2097152 | tf_op jit(solution)/shard_map/pallas_call | solution.py:189
  46.9 15.3 %all-to-all-done.1.back_ref = bf16[64,32,128]{2,1,0:T(8,128)(2,1)S(1)} async-done(((bf16[64,32,128]{2,1,0:T(8,128)(2,1)}), bf16[64,32,128]{2,1,0:T(8,128)(2,1)S(1)}, u32[]{:S(2)}, u32[]{:S(2)}) %all-to-all-start.1) | async-done | bytes 524320 | tf_op jit(solution)/shard_map/all_to_all | solution.py:213
  62.2 3.0 %shard_map.87 = (bf16[128,1024]{1,0:T(8,128)(2,1)}, f32[16,128]{1,0:T(8,128)}, bf16[8,256,128]{2,1,0:T(8,128)(2,1)S(1)}) custom-call(bf16[64,32,128]{2,1,0:T(8,128)(2,1)S(1)} %all-to-all-done.1.back_ref, bf16[128,1024]{1,0:T(8,128)(2,1)S(1)} %copy-done.1, bf16[128,128]{1,0:T(8,128)(2,1)S(1)} %copy-done.5, bf16[128,128]{1,0:T(8,128)(2,1)S(1)} %copy-done.7, ...), custom_call_target="tpu_custom_call" | custom-call | flops 268435456 | bytes 2097152 | tf_op jit(solution)/shard_map/pallas_call | solution.py:189
  65.1 27.1 %all_to_all.16 = bf16[8,256,128]{2,1,0:T(8,128)(2,1)S(1)} all-to-all(bf16[8,256,128]{2,1,0:T(8,128)(2,1)S(1)} %get-tuple-element.20), channel_id=1, replica_groups=mesh['seq'=64,'head'=8] {'head'}, dimensions={0} | all-to-all | bytes 1048576 | tf_op jit(solution)/shard_map/all_to_all | solution.py:220
  92.3 0.1 reduce_sum.12
  92.3 0.6 fusion
Async XLA Ops:
  0.6 1.0 %copy-start = (bf16[128,1024]{1,0:T(8,128)(2,1)S(1)}, bf16[128,1024]{1,0:T(8,128)(2,1)}, u32[]{:S(2)}) copy-start(bf16[128,1024]{1,0:T(8,128)(2,1)} %x_ref.5) | copy-start | bytes 786436
  1.6 0.9 %copy-start.2 = (bf16[128,1024]{1,0:T(8,128)(2,1)S(1)}, bf16[128,1024]{1,0:T(8,128)(2,1)}, u32[]{:S(2)}) copy-start(bf16[128,1024]{1,0:T(8,128)(2,1)} %grad_ref.5) | copy-start | bytes 786436
  2.5 0.8 copy-start.4
  3.3 0.8 copy-start.6
  4.1 0.7 copy-start.8
  38.4 6.4 %copy-start.1 = (bf16[128,1024]{1,0:T(8,128)(2,1)S(1)}, bf16[128,1024]{1,0:T(8,128)(2,1)}, u32[]{:S(2)}) copy-start(bf16[128,1024]{1,0:T(8,128)(2,1)} %x_ref.5) | copy-start | bytes 786436
  38.4 6.4 %copy-start.3 = (bf16[128,1024]{1,0:T(8,128)(2,1)S(1)}, bf16[128,1024]{1,0:T(8,128)(2,1)}, u32[]{:S(2)}) copy-start(bf16[128,1024]{1,0:T(8,128)(2,1)} %grad_ref.5) | copy-start | bytes 786436
  38.4 6.5 %copy-start.5 = (bf16[128,128]{1,0:T(8,128)(2,1)S(1)}, bf16[128,128]{1,0:T(8,128)(2,1)}, u32[]{:S(2)}) copy-start(bf16[128,128]{1,0:T(8,128)(2,1)} %b_ref.5) | copy-start | bytes 98308
  38.4 6.5 %copy-start.7 = (bf16[128,128]{1,0:T(8,128)(2,1)S(1)}, bf16[128,128]{1,0:T(8,128)(2,1)}, u32[]{:S(2)}) copy-start(bf16[128,128]{1,0:T(8,128)(2,1)} %c_ref.5) | copy-start | bytes 98308
  38.4 6.5 %copy-start.9 = (f32[16,128]{1,0:T(8,128)S(1)}, f32[16,128]{1,0:T(8,128)}, u32[]{:S(2)}) copy-start(f32[16,128]{1,0:T(8,128)} %log_ref.5) | copy-start | bytes 24580
  38.4 23.7 %all-to-all-start.1 = ((bf16[64,32,128]{2,1,0:T(8,128)(2,1)}), bf16[64,32,128]{2,1,0:T(8,128)(2,1)S(1)}, u32[]{:S(2)}, u32[]{:S(2)}) async-start(bf16[64,32,128]{2,1,0:T(8,128)(2,1)} %shard_map.85), calls=%async_computation.1 | async-start | bytes 1048576 | tf_op jit(solution)/shard_map/all_to_all | solution.py:213

commit v2 on v1

v2 whole, which is shorter than its diff:
```python
import functools

import jax
import jax.numpy as jnp
from jax import lax
from jax.experimental import pallas as pl
from jax.experimental.pallas import tpu as pltpu
from jax.sharding import PartitionSpec as P

F32 = jnp.float32
BF16 = jnp.bfloat16
HIGHEST = lax.Precision.HIGHEST
TOK = 128
LANES = 128
HALF = 64
HEADS = 16
WIDE = HEADS * HALF
PAIRS = 8
CHUNKS = 8
ROWS = 16
SEND_ROWS = 2 * ROWS + 8
TAIL = 16


def nn(a, b, precision=None):
    return lax.dot_general(
        a, b, (((1,), (0,)), ((), ())), precision=precision, preferred_element_type=F32
    )


def nt(a, b, precision=None):
    return lax.dot_general(
        a, b, (((1,), (1,)), ((), ())), precision=precision, preferred_element_type=F32
    )


def iota(dim, shape=(TOK, LANES)):
    return lax.broadcasted_iota(jnp.int32, shape, dim)


def pair(g):
    return slice(g * LANES, (g + 1) * LANES)


def transposed(matrix):
    return matrix.astype(F32).T.astype(BF16)


def split(value):
    high = value.astype(BF16)
    return high, (value - high.astype(F32)).astype(BF16)


def cumulative_columns(log_decay):
    lower = (iota(0) >= iota(1)).astype(F32)
    return nt(lower, log_decay, HIGHEST)


def spread(columns, g):
    rows = columns.shape[0]
    left = iota(1, (rows, LANES)) < HALF
    a = jnp.broadcast_to(columns[:, 2 * g : 2 * g + 1], (rows, LANES))
    b = jnp.broadcast_to(columns[:, 2 * g + 1 : 2 * g + 2], (rows, LANES))
    return jnp.where(left, a, b)


def core():
    return lax.axis_index("seq") % 2


def first_core(shape):
    return jnp.full(shape, core(), jnp.int32) == 0


def half_pair(half, i):
    return pl.ds(pl.multiple_of(half * (WIDE // 2) + i * LANES, LANES), LANES)


def two_rows(value, rows):
    wide = jnp.broadcast_to(value, (rows, LANES))
    high = wide.astype(BF16).astype(F32)
    return jnp.where(iota(0, (rows, LANES)) == 0, high, wide - high).astype(BF16)


def one_row(rows):
    rows = rows.astype(F32)
    return rows[0:1, :] + rows[1:2, :]


def load(pairs, sems):
    copies = [pltpu.make_async_copy(a, b, sems.at[i]) for i, (a, b) in enumerate(pairs)]
    for copy in copies:
        copy.start()
    return copies


def states_kernel(
    x_hbm, b_hbm, c_hbm, log_hbm, grad_hbm,
    send_ref, mine_ref, factor_ref,
    x_ref, b_ref, c_ref, log_ref, grad_ref, sems,
):
    copies = load(
        [(log_hbm, log_ref), (b_hbm, b_ref), (c_hbm, c_ref), (x_hbm, x_ref), (grad_hbm, grad_ref)],
        sems,
    )
    copies[0].wait()
    cum = cumulative_columns(log_ref[...])
    total = cum[TOK - 1 : TOK, :]
    to_end = jnp.exp(total - cum)
    from_start = jnp.exp(cum)
    last = jnp.exp(total)
    copies[1].wait()
    b_t = transposed(b_ref[...])
    copies[2].wait()
    c_t = transposed(c_ref[...])
    copies[3].wait()
    copies[4].wait()
    for g in range(PAIRS):
        wx = (x_ref[:, pair(g)].astype(F32) * spread(to_end, g)).astype(BF16)
        wg = (grad_ref[:, pair(g)].astype(F32) * spread(from_start, g)).astype(BF16)
        ends = nn(b_t, wx)
        opens = nn(c_t, wg)
        factor = spread(last, g)
        mine_ref[0:TOK, pair(g)] = ends
        mine_ref[TOK : 2 * TOK, pair(g)] = opens
        send_ref[0:TOK, pair(g)] = ends.astype(BF16)
        send_ref[TOK : 2 * TOK, pair(g)] = opens.astype(BF16)
        send_ref[2 * TOK : 2 * TOK + TAIL, pair(g)] = two_rows(factor, TAIL)
        factor_ref[:, pair(g)] = jnp.broadcast_to(factor, (8, LANES))


def chip_kernel(got_ref, mine_ref, factor_ref, send_ref):
    half = core()
    first = first_core((TOK, LANES))
    first_row = first_core((1, LANES))
    for i in range(PAIRS // 2):
        lanes = half_pair(half, i)
        mine = factor_ref[0:1, lanes]
        theirs = one_row(got_ref[2 * TOK : 2 * TOK + TAIL, lanes])
        factor0 = jnp.where(first_row, mine, theirs)
        factor1 = jnp.where(first_row, theirs, mine)
        my_ends = mine_ref[0:TOK, lanes]
        my_opens = mine_ref[TOK : 2 * TOK, lanes]
        ends = got_ref[0:TOK, lanes].astype(F32)
        opens = got_ref[TOK : 2 * TOK, lanes].astype(F32)
        chip_ends = factor1 * jnp.where(first, my_ends, ends) + jnp.where(first, ends, my_ends)
        chip_opens = factor0 * jnp.where(first, opens, my_opens) + jnp.where(first, my_opens, opens)
        chip_ends = chip_ends.astype(BF16)
        chip_opens = chip_opens.astype(BF16)
        factors = two_rows(mine * theirs, 8)
        for r in range(CHUNKS):
            rows = slice(r * ROWS, (r + 1) * ROWS)
            send_ref[i * CHUNKS + r] = jnp.concatenate(
                [chip_ends[rows], chip_opens[rows], factors], axis=0
            )


def recurrence_kernel(got_ref, back_ref):
    count = got_ref.shape[0]
    entry = jnp.zeros((ROWS, LANES), F32)
    adjoint = jnp.zeros((ROWS, LANES), F32)
    entries, adjoints = [None] * count, [None] * count
    for k in range(count):
        m = count - 1 - k
        entries[k], adjoints[m] = entry, adjoint
        entry = one_row(got_ref[k, 2 * ROWS : SEND_ROWS]) * entry + got_ref[k, 0:ROWS].astype(F32)
        adjoint = one_row(got_ref[m, 2 * ROWS : SEND_ROWS]) * adjoint + got_ref[
            m, ROWS : 2 * ROWS
        ].astype(F32)
    for k in range(count):
        overlap = jnp.sum(entries[k] * adjoints[k], axis=0, keepdims=True)
        back_ref[k] = jnp.concatenate(
            [entries[k].astype(BF16), adjoints[k].astype(BF16), two_rows(overlap, 8)], axis=0
        )


def intra_kernel(
    x_hbm, b_hbm, c_hbm, log_hbm, grad_hbm,
    gx_ref, decay_ref, bc_ref, wx_ref, wg_ref, mats_ref, end_ref,
    x_ref, b_ref, c_ref, log_ref, grad_ref, sems,
):
    copies = load(
        [(log_hbm, log_ref), (b_hbm, b_ref), (c_hbm, c_ref), (x_hbm, x_ref), (grad_hbm, grad_ref)],
        sems,
    )
    for copy in copies:
        copy.wait()
    log_decay = log_ref[...]
    upper = (iota(0) <= iota(1)).astype(F32)
    cum_rows = nn(log_decay, upper, HIGHEST)
    cum = cumulative_columns(log_decay)
    to_end = jnp.exp(cum[TOK - 1 : TOK, :] - cum)
    from_start = jnp.exp(cum)
    b_mat = b_ref[...]
    c_mat = c_ref[...]
    mats_ref[0] = b_mat
    mats_ref[1] = c_mat
    scores = nt(b_mat, c_mat)
    later = iota(1) >= iota(0)
    before = iota(0) < iota(1)
    ends_after = (iota(0) >= iota(1)).astype(BF16)
    left = iota(1) < HALF
    mixed_sum = jnp.zeros((TOK, TOK), F32)
    for g in range(PAIRS):
        x_g = x_ref[:, pair(g)]
        grad_g = grad_ref[:, pair(g)]
        end_g = spread(to_end, g)
        end_ref[:, pair(g)] = end_g
        wx_ref[:, pair(g)] = (x_g.astype(F32) * end_g).astype(BF16)
        wg_ref[:, pair(g)] = (grad_g.astype(F32) * spread(from_start, g)).astype(BF16)
        grad_x = jnp.zeros((TOK, LANES), F32)
        for j in range(2):
            h = 2 * g + j
            mine = left if j == 0 else jnp.logical_not(left)
            x_h = jnp.where(mine, x_g, jnp.zeros_like(x_g))
            grad_h = jnp.where(mine, grad_g, jnp.zeros_like(grad_g))
            pairs = nt(x_h, grad_g)
            gaps = cum_rows[h : h + 1, :] - cum[:, h : h + 1]
            decays = jnp.exp(jnp.where(later, gaps, -1e4))
            kernel = decays * scores
            mixed_sum = mixed_sum + decays * pairs
            grad_x = grad_x + nn(kernel.astype(BF16), grad_h)
            reach = nn((kernel * pairs).astype(BF16), ends_after)
            decay_ref[h : h + 1, :] = jnp.sum(
                jnp.where(before, reach, 0.0), axis=0, keepdims=True
            )
        gx_ref[:, pair(g)] = grad_x
    high, low = split(mixed_sum)
    high_t, low_t = split(mixed_sum.T)
    bc_ref[0] = nn(high, c_mat) + nn(low, c_mat)
    bc_ref[1] = nn(high_t, b_mat) + nn(low_t, b_mat)


def slices(ref, i, start, rows):
    return ref[i * CHUNKS : (i + 1) * CHUNKS, start : start + rows, :]


def half_sums(half, back_ref, got_ref, wx_ref, wg_ref, b_sum, c_sum, state_ref):
    first = first_core((TOK, LANES))
    for i in range(PAIRS // 2):
        lanes = half_pair(half, i)
        theirs = one_row(got_ref[2 * TOK : 2 * TOK + TAIL, lanes])
        entry = slices(back_ref, i, 0, ROWS).reshape(TOK, LANES)
        adjoint = slices(back_ref, i, ROWS, ROWS).reshape(TOK, LANES)
        inside = jnp.where(first, adjoint.astype(F32), entry.astype(F32)) * theirs
        added = jnp.where(
            first, got_ref[TOK : 2 * TOK, lanes].astype(F32), got_ref[0:TOK, lanes].astype(F32)
        )
        inside = inside + added
        entry = jnp.where(first, entry.astype(F32), inside).astype(BF16)
        adjoint = jnp.where(first, inside, adjoint.astype(F32)).astype(BF16)
        state_ref[0, :, i * LANES : (i + 1) * LANES] = entry
        state_ref[1, :, i * LANES : (i + 1) * LANES] = adjoint
        b_sum = b_sum + nt(wx_ref[:, lanes], adjoint)
        c_sum = c_sum + nt(wg_ref[:, lanes], entry)
    return b_sum, c_sum


def own_kernel(back_ref, got_ref, wx_ref, wg_ref, bc_ref, state_ref, part_ref):
    part_ref[0], part_ref[1] = half_sums(
        core(), back_ref, got_ref, wx_ref, wg_ref, bc_ref[0], bc_ref[1], state_ref
    )


def other_kernel(back_ref, got_ref, wx_ref, wg_ref, part_ref, state_ref, send_ref):
    b_sum, c_sum = half_sums(
        1 - core(), back_ref, got_ref, wx_ref, wg_ref, part_ref[0], part_ref[1], state_ref
    )
    b_out = b_sum.astype(BF16)
    c_out = c_sum.astype(BF16)
    for z in range(send_ref.shape[0]):
        send_ref[z, 0:TOK, :] = b_out
        send_ref[z, TOK : 2 * TOK, :] = c_out


def grads_kernel(
    own_ref, other_ref, own_state_ref, other_state_ref, got_ref, factor_ref,
    wx_ref, wg_ref, mats_ref, gx_ref, inner_ref, end_ref,
    out_ref, decay_ref,
):
    first = first_core((TOK, LANES))
    b_mat = mats_ref[0]
    c_mat = mats_ref[1]
    last = iota(0) == TOK - 1
    alphas = jnp.zeros((TOK, LANES), F32)
    betas = jnp.zeros((TOK, LANES), F32)
    for half, back_ref, state_ref in (
        (core(), own_ref, own_state_ref),
        (1 - core(), other_ref, other_state_ref),
    ):
        for i in range(PAIRS // 2):
            lanes = half_pair(half, i)
            entry = state_ref[0, :, i * LANES : (i + 1) * LANES]
            adjoint = state_ref[1, :, i * LANES : (i + 1) * LANES]
            from_adjoint = nn(b_mat, adjoint)
            out_ref[:, lanes] = (gx_ref[:, lanes] + end_ref[:, lanes] * from_adjoint).astype(BF16)
            beta = wx_ref[:, lanes].astype(F32) * from_adjoint
            alpha = wg_ref[:, lanes].astype(F32) * nn(c_mat, entry)
            chip = one_row(jnp.sum(slices(back_ref, i, 2 * ROWS, 8).astype(F32), axis=0))
            outer = jnp.where(
                first,
                slices(back_ref, i, 0, ROWS).reshape(TOK, LANES).astype(F32)
                * got_ref[TOK : 2 * TOK, lanes].astype(F32),
                slices(back_ref, i, ROWS, ROWS).reshape(TOK, LANES).astype(F32)
                * got_ref[0:TOK, lanes].astype(F32),
            )
            theirs = one_row(got_ref[2 * TOK : 2 * TOK + TAIL, lanes])
            constant = factor_ref[0:1, lanes] * (
                theirs * chip + jnp.sum(outer, axis=0, keepdims=True)
            )
            alpha = alpha + jnp.where(last, constant, 0.0)
            head = 2 * (half * (PAIRS // 2) + i)
            pick = (iota(1) == head + iota(0) // HALF).astype(BF16)
            beta_high, beta_low = split(beta)
            alpha_high, alpha_low = split(alpha)
            betas = betas + nn(beta_high, pick) + nn(beta_low, pick)
            alphas = alphas + nn(alpha_high, pick) + nn(alpha_low, pick)
    after = (iota(0) <= iota(1)).astype(F32)
    before = (iota(0) > iota(1)).astype(F32)
    decay = nn(after, alphas, HIGHEST) + nn(before, betas, HIGHEST)
    decay_ref[...] = inner_ref[...] + decay.T[0:HEADS, :]


def head_sum_kernel(parts_ref, b_ref, c_ref):
    b_ref[...] = jnp.sum(parts_ref[:, 0:TOK, :].astype(F32), axis=0).astype(BF16)
    c_ref[...] = jnp.sum(parts_ref[:, TOK : 2 * TOK, :].astype(F32), axis=0).astype(BF16)


HBM_SPEC = pl.BlockSpec(memory_space=pltpu.HBM)


def call(body, outs, micros, *args, from_hbm=False, scratch=()):
    more = {}
    if from_hbm:
        more["in_specs"] = [HBM_SPEC] * len(args)
        args = [pltpu.with_memory_space_constraint(a, pltpu.HBM) for a in args]
    return pl.pallas_call(
        body,
        out_shape=[jax.ShapeDtypeStruct(s, d) for s, d in outs],
        scratch_shapes=list(scratch),
        compiler_params=pltpu.CompilerParams(vmem_limit_bytes=24 * 1024 * 1024),
        cost_estimate=pl.CostEstimate(
            flops=int(micros * 1e9), bytes_accessed=1 << 18, transcendentals=0
        ),
        **more,
    )(*args)


def per_device(seq, heads, x, b_mat, c_mat, log_decay, grad):
    chips = seq // 2
    assert chips == PAIRS // 2 * CHUNKS
    inputs = (x, b_mat, c_mat, log_decay, grad)
    swap = [(i, i ^ 1) for i in range(seq)]
    same_core = [[2 * m + c for m in range(chips)] for c in range(2)]
    wide = (TOK, WIDE)
    half_state = ((2, TOK, WIDE // 2), BF16)
    loaded = (
        pltpu.VMEM(wide, BF16),
        pltpu.VMEM((TOK, LANES), BF16),
        pltpu.VMEM((TOK, LANES), BF16),
        pltpu.VMEM((HEADS, TOK), F32),
        pltpu.VMEM(wide, BF16),
        pltpu.SemaphoreType.DMA((5,)),
    )
    send, mine, factor = call(
        states_kernel,
        [((2 * TOK + TAIL, WIDE), BF16), ((2 * TOK, WIDE), F32), ((8, WIDE), F32)],
        1,
        *inputs,
        from_hbm=True,
        scratch=loaded,
    )
    got = lax.ppermute(send, "seq", swap)
    (send,) = call(chip_kernel, [((chips, SEND_ROWS, LANES), BF16)], 1, got, mine, factor)
    gathered = lax.all_to_all(send, "seq", 0, 0, tiled=True, axis_index_groups=same_core)
    local = call(
        intra_kernel,
        [
            (wide, F32),
            ((HEADS, TOK), F32),
            ((2, TOK, LANES), F32),
            (wide, BF16),
            (wide, BF16),
            ((2, TOK, LANES), BF16),
            (wide, F32),
        ],
        3,
        *inputs,
        from_hbm=True,
        scratch=loaded,
    )
    gathered, (gx, inner, bc, wx, wg, mats, end) = lax.optimization_barrier((gathered, local))
    (back,) = call(recurrence_kernel, [((chips, SEND_ROWS, LANES), BF16)], 1, gathered)
    back = lax.all_to_all(back, "seq", 0, 0, tiled=True, axis_index_groups=same_core)
    other = lax.ppermute(back, "seq", swap)
    own_state, part = call(
        own_kernel, [half_state, ((2, TOK, LANES), F32)], 1, back, got, wx, wg, bc
    )
    other_state, parts = call(
        other_kernel,
        [half_state, ((heads, 2 * TOK, LANES), BF16)],
        1, other, got, wx, wg, part,
    )
    parts = lax.all_to_all(parts, "head", 0, 0, tiled=True)
    grad_x, decay_grad = call(
        grads_kernel,
        [(wide, BF16), ((HEADS, TOK), F32)],
        3,
        back, other, own_state, other_state, got, factor, wx, wg, mats, gx, inner, end,
    )
    parts, grad_x, decay_grad = lax.optimization_barrier((parts, grad_x, decay_grad))
    grad_b, grad_c = call(head_sum_kernel, [((TOK, LANES), BF16)] * 2, 1, parts)
    return grad_x, grad_b, grad_c, decay_grad


def solution(mesh):
    in_specs = (
        P("seq", "head"),
        P("seq", None),
        P("seq", None),
        P("head", "seq"),
        P("seq", "head"),
    )
    out_specs = (P("seq", "head"), P("seq", None), P("seq", None), P("head", "seq"))
    return jax.shard_map(
        functools.partial(per_device, mesh.shape["seq"], mesh.shape["head"]),
        mesh=mesh,
        in_specs=in_specs,
        out_specs=out_specs,
        check_vma=False,
    )
```

time: 93.5 us -> 84 us (0.90)
  blocking collectives: 58.7 us -> 17.3 us
  starting transfers between devices: 6.4 us -> 29.5 us
  waiting for transfers between devices: 15.3 us -> 23.5 us
  Pallas kernels: 7.05 us -> 10.8 us
  local copies, waits for them, and re-layouts: 4.76 us -> 1.83 us
    all_to_all x2 -> x1, blocking collectives: 58.7 us -> 17.3 us  [per_device(): lax.all_to_all(back, 'seq', 0, 0, tiled=True, axis_index_groups=same_core)]
    ppermute x0 -> x2, starting transfers between devices: none -> 15.1 us  [the longest x1 8.79 us: per_device(): got = lax.ppermute(send, 'seq', swap)]
    all_to_all x1 -> x2, starting transfers between devices: 6.4 us -> 14.3 us  [the longest x1 10 us: per_device(): parts = lax.all_to_all(parts, 'head', 0, 0, tiled=True)]
    all_to_all x1 -> x2, waiting for transfers between devices: 15.3 us -> 21.1 us  [the longest x1 14.6 us: per_device(): parts = lax.all_to_all(parts, 'head', 0, 0, tiled=True)]
    pallas_call x4 -> x8, Pallas kernels: 7.05 us -> 10.8 us  [call(): pl.pallas_call(body, out_shape=[jax.ShapeDtypeStruct(s, d) for s, d in ou...]
    ppermute x0 -> x2, waiting for transfers between devices: none -> 2.46 us  [the longest x1 1.56 us: per_device(): got = lax.ppermute(send, 'seq', swap)]
    unnamed x20 -> x4, local copies, waits for them, and re-layouts: 4.13 us -> 1.83 us
  transfers between devices with their start and end apart: 1 -> 4, of which waited for: 1 -> 4; matrix products, arithmetic and copies ran while one was open for 0% -> 0% of each run, Pallas kernels for 2% -> 7%
where the time goes in v2:
time: 84 us; the launch traced here: 83.6 us
  starting transfers between devices  29.5 us (35%)
  waiting for transfers between devices  23.5 us (28%)
  blocking collectives  17.3 us (21%)
  Pallas kernels  10.8 us (13%)
  local copies, waits for them, and re-layouts  1.83 us (2%)
    all_to_all x1, blocking collectives, per_device(): lax.all_to_all(back, 'seq', 0, 0, tiled=True, axis_index_groups=same_core)  17.3 us
    all_to_all x1, waiting for transfers between devices, per_device(): parts = lax.all_to_all(parts, 'head', 0, 0, tiled=True)  14.6 us
    pallas_call x8, Pallas kernels, call(): pl.pallas_call(body, out_shape=[jax.ShapeDtypeStruct(s, d) for s, d in ou...  10.8 us
    all_to_all x1, starting transfers between devices, per_device(): parts = lax.all_to_all(parts, 'head', 0, 0, tiled=True)  10 us
    ppermute x1, starting transfers between devices, per_device(): got = lax.ppermute(send, 'seq', swap)  8.79 us
    all_to_all x1, waiting for transfers between devices, per_device(): lax.all_to_all(send, 'seq', 0, 0, tiled=True, axis_index_groups=same_core)  6.5 us
    ppermute x1, starting transfers between devices, per_device(): other = lax.ppermute(back, 'seq', swap)  6.36 us
    all_to_all x1, starting transfers between devices, per_device(): lax.all_to_all(send, 'seq', 0, 0, tiled=True, axis_index_groups=same_core)  4.3 us
  transfers between devices with their start and end apart: 4, of which 4 were waited for; matrix products, arithmetic and copies ran while one was open for 0% of the time, Pallas kernels for 7%

profile of v2, /device:TPU:1, one launch (start us, length us, event | category | flops | bytes accessed | tf_op | source)
XLA Modules:
  0.0 83.6 jit_solution(121003576575484849)
XLA Ops:
  0.6 2.1 %shard_map.84 = (bf16[272,1024]{1,0:T(8,128)(2,1)S(1)}, f32[256,1024]{1,0:T(8,128)S(1)}, f32[8,1024]{1,0:T(8,128)S(1)}) custom-call(bf16[128,1024]{1,0:T(8,128)(2,1)} %x_hbm.3, bf16[128,128]{1,0:T(8,128)(2,1)} %b_hbm.3, bf16[128,128]{1,0:T(8,128)(2,1)} %c_hbm.3, f32[16,128]{1,0:T(8,128)} %log_hbm.3, bf16[128,1024]{1,0:T(8,128)(2,1)} %grad_hbm.3), custom_call_target="tpu_custom_call" | custom-call | flops 1000000000 | bytes 262144 | tf_op jit(solution)/shard_map/pallas_call | solution.py:337
  2.7 8.8 %collective-permute-start = (bf16[272,1024]{1,0:T(8,128)(2,1)S(1)}, bf16[272,1024]{1,0:T(8,128)(2,1)S(1)}, u32[]{:S(2)}, u32[]{:S(2)}) collective-permute-start(bf16[272,1024]{1,0:T(8,128)(2,1)S(1)} %get-tuple-element.33), channel_id=1, source_target_pairs={{0,8},{8,0},{16,24},{24,16},{32,40},{40,32},{48,56},{56,48},{64,72... | collective-permute-start | bytes 1671176 | tf_op jit(solution)/shard_map/ppermute | solution.py:373
  11.5 1.6 %collective-permute-done.got_ref = bf16[272,1024]{1,0:T(8,128)(2,1)S(1)} collective-permute-done((bf16[272,1024]{1,0:T(8,128)(2,1)S(1)}, bf16[272,1024]{1,0:T(8,128)(2,1)S(1)}, u32[]{:S(2)}, u32[]{:S(2)}) %collective-permute-start) | collective-permute-done | bytes 557088 | tf_op jit(solution)/shard_map/ppermute | solution.py:373
  13.1 0.9 %shard_map.85 = bf16[32,40,128]{2,1,0:T(8,128)(2,1)} custom-call(bf16[272,1024]{1,0:T(8,128)(2,1)S(1)} %collective-permute-done.got_ref, f32[256,1024]{1,0:T(8,128)S(1)} %get-tuple-element.34.mine_ref, f32[8,1024]{1,0:T(8,128)S(1)} %get-tuple-element.35.factor_ref), custom_call_target="tpu_custom_call" | custom-call | flops 1000000000 | bytes 262144 | tf_op jit(solution)/shard_map/pallas_call | solution.py:337
  14.0 4.3 %all-to-all-start = ((bf16[32,40,128]{2,1,0:T(8,128)(2,1)}), bf16[32,40,128]{2,1,0:T(8,128)(2,1)S(1)}, u32[]{:S(2)}, u32[]{:S(2)}) async-start(bf16[32,40,128]{2,1,0:T(8,128)(2,1)} %shard_map.85), calls=%async_computation | async-start | bytes 655360 | tf_op jit(solution)/shard_map/all_to_all | solution.py:375
  18.3 3.2 %shard_map.86 = (f32[128,1024]{1,0:T(8,128)S(1)}, f32[16,128]{1,0:T(8,128)S(1)}, f32[2,128,128]{2,1,0:T(8,128)S(1)}, bf16[128,1024]{1,0:T(8,128)(2,1)S(1)}, bf16...) custom-call(bf16[128,1024]{1,0:T(8,128)(2,1)} %x_hbm.3, ...), custom_call_target="tpu_custom_call" | custom-call | flops 3000000000 | bytes 262144 | tf_op jit(solution)/shard_map/pallas_call | solution.py:337
  21.4 0.0 copy-start
  21.4 0.8 copy-done
  22.2 6.5 %all-to-all-done.got_ref = bf16[32,40,128]{2,1,0:T(8,128)(2,1)S(1)} async-done(((bf16[32,40,128]{2,1,0:T(8,128)(2,1)}), bf16[32,40,128]{2,1,0:T(8,128)(2,1)S(1)}, u32[]{:S(2)}, u32[]{:S(2)}) %all-to-all-start) | async-done | bytes 327712 | tf_op jit(solution)/shard_map/all_to_all | solution.py:375
  28.7 0.2 shard_map.87
  28.9 17.3 %all_to_all.15.back_ref.own_ref = bf16[32,40,128]{2,1,0:T(8,128)(2,1)S(1)} all-to-all(bf16[32,40,128]{2,1,0:T(8,128)(2,1)S(1)} %shard_map.87), channel_id=1, replica_groups={{0,16,32,48,64,80,96,112,128,144,160,176,192,208,224,240,256,272,288,30..., dimensions={0} | all-to-all | bytes 655360 | tf_op jit(solution)/shard_map/all_to_all | solution.py:394
  46.2 6.4 %collective-permute-start.1 = (bf16[32,40,128]{2,1,0:T(8,128)(2,1)S(1)}, bf16[32,40,128]{2,1,0:T(8,128)(2,1)S(1)}, u32[]{:S(2)}, u32[]{:S(2)}) collective-permute-start(bf16[32,40,128]{2,1,0:T(8,128)(2,1)S(1)} %all_to_all.15.back_ref.own_ref), channel_id=1, source_target_pairs={{0,8},{8,0},{16,24},{24,16},{32,40},{40,32},{48,56},{56,48},{64,72... | collective-permute-start | bytes 983048 | tf_op jit(solution)/shard_map/ppermute | solution.py:395
  52.5 0.3 shard_map.88
  52.9 0.9 %collective-permute-done.1.back_ref.other_ref = bf16[32,40,128]{2,1,0:T(8,128)(2,1)S(1)} collective-permute-done((bf16[32,40,128]{2,1,0:T(8,128)(2,1)S(1)}, bf16[32,40,128]{2,1,0:T(8,128)(2,1)S(1)}, u32[]{:S(2)}, u32[]{:S(2)}) %collective-permute-start.1) | collective-permute-done | bytes 327712 | tf_op jit(solution)/shard_map/ppermute | solution.py:395
  53.8 1.2 %shard_map.89 = (bf16[2,128,512]{2,1,0:T(8,128)(2,1)S(1)}, bf16[8,256,128]{2,1,0:T(8,128)(2,1)}) custom-call(bf16[32,40,128]{2,1,0:T(8,128)(2,1)S(1)} %collective-permute-done.1.back_ref.other_ref, bf16[272,1024]{1,0:T(8,128)(2,1)S(1)} %collective-permute-done.got_ref, bf16[128,1024]{1,0:T(8,128)(2,1)S(1)} %get-tuple-element.44.wx_ref, ...), custom_call_target="tpu_custom_call" | custom-call | flops 1000000000 | bytes 262144 | tf_op jit(solution)/shard_map/pallas_call | solution.py:337
  54.9 10.0 %all-to-all-start.2 = ((bf16[8,256,128]{2,1,0:T(8,128)(2,1)}), bf16[8,256,128]{2,1,0:T(8,128)(2,1)S(1)}, u32[]{:S(2)}, u32[]{:S(2)}) async-start(bf16[8,256,128]{2,1,0:T(8,128)(2,1)} %get-tuple-element.48), calls=%async_computation.2 | async-start | bytes 1048576 | tf_op jit(solution)/shard_map/all_to_all | solution.py:404
  65.0 0.0 copy-start.1
  65.0 1.0 %copy-done.1 = f32[128,1024]{1,0:T(8,128)S(1)} copy-done((f32[128,1024]{1,0:T(8,128)S(1)}, f32[128,1024]{1,0:T(8,128)}, u32[]{:S(2)}) %copy-start.1) | copy-done | bytes 524312
  66.0 2.4 %shard_map.90 = (bf16[128,1024]{1,0:T(8,128)(2,1)}, f32[16,128]{1,0:T(8,128)}) custom-call(bf16[32,40,128]{2,1,0:T(8,128)(2,1)S(1)} %all_to_all.15.back_ref.own_ref, bf16[32,40,128]{2,1,0:T(8,128)(2,1)S(1)} %collective-permute-done.1.back_ref.other_ref, bf16[2,128,512]{2,1,0:T(8,128)(2,1)S(1)} %get-tuple-element.49.own_state_ref, ...), custom_call_target="tpu_custom_call" | custom-call | flops 3000000000 | bytes 262144 | tf_op jit(solution)/shard_map/pallas_call | solution.py:337
  68.4 14.6 %all-to-all-done.2.parts_ref = bf16[8,256,128]{2,1,0:T(8,128)(2,1)S(1)} async-done(((bf16[8,256,128]{2,1,0:T(8,128)(2,1)}), bf16[8,256,128]{2,1,0:T(8,128)(2,1)S(1)}, u32[]{:S(2)}, u32[]{:S(2)}) %all-to-all-start.2) | async-done | bytes 524320 | tf_op jit(solution)/shard_map/all_to_all | solution.py:404
  82.9 0.7 shard_map.91
Async XLA Ops:
  2.7 10.4 %collective-permute-start = (bf16[272,1024]{1,0:T(8,128)(2,1)S(1)}, bf16[272,1024]{1,0:T(8,128)(2,1)S(1)}, u32[]{:S(2)}, u32[]{:S(2)}) collective-permute-start(bf16[272,1024]{1,0:T(8,128)(2,1)S(1)} %get-tuple-element.33), channel_id=1, source_target_pairs={{0,8},{8,0},{16,24},{24,16},{32,40},{40,32},{48,56},{56,48},{64,72... | collective-permute-start | bytes 1671176 | tf_op jit(solution)/shard_map/ppermute | solution.py:373
  14.0 14.8 %all-to-all-start = ((bf16[32,40,128]{2,1,0:T(8,128)(2,1)}), bf16[32,40,128]{2,1,0:T(8,128)(2,1)S(1)}, u32[]{:S(2)}, u32[]{:S(2)}) async-start(bf16[32,40,128]{2,1,0:T(8,128)(2,1)} %shard_map.85), calls=%async_computation | async-start | bytes 655360 | tf_op jit(solution)/shard_map/all_to_all | solution.py:375
  21.4 0.8 copy-start
  46.2 7.6 %collective-permute-start.1 = (bf16[32,40,128]{2,1,0:T(8,128)(2,1)S(1)}, bf16[32,40,128]{2,1,0:T(8,128)(2,1)S(1)}, u32[]{:S(2)}, u32[]{:S(2)}) collective-permute-start(bf16[32,40,128]{2,1,0:T(8,128)(2,1)S(1)} %all_to_all.15.back_ref.own_ref), channel_id=1, source_target_pairs={{0,8},{8,0},{16,24},{24,16},{32,40},{40,32},{48,56},{56,48},{64,72... | collective-permute-start | bytes 983048 | tf_op jit(solution)/shard_map/ppermute | solution.py:395
  54.9 28.0 %all-to-all-start.2 = ((bf16[8,256,128]{2,1,0:T(8,128)(2,1)}), bf16[8,256,128]{2,1,0:T(8,128)(2,1)S(1)}, u32[]{:S(2)}, u32[]{:S(2)}) async-start(bf16[8,256,128]{2,1,0:T(8,128)(2,1)} %get-tuple-element.48), calls=%async_computation.2 | async-start | bytes 1048576 | tf_op jit(solution)/shard_map/all_to_all | solution.py:404
  65.0 1.0 %copy-start.1 = (f32[128,1024]{1,0:T(8,128)S(1)}, f32[128,1024]{1,0:T(8,128)}, u32[]{:S(2)}) copy-start(f32[128,1024]{1,0:T(8,128)} %copy-done) | copy-start | bytes 1572868

commit v3 on v2

--- a/solution.py
+++ b/solution.py
@@ -15,6 +15,7 @@
 HALF = 64
 HEADS = 16
 WIDE = HEADS * HALF
+HALF_WIDE = WIDE // 2
 PAIRS = 8
 CHUNKS = 8
 ROWS = 16
@@ -72,8 +73,12 @@
     return jnp.full(shape, core(), jnp.int32) == 0
 
 
+def half_lanes(half):
+    return pl.ds(pl.multiple_of(half * HALF_WIDE, HALF_WIDE), HALF_WIDE)
+
+
 def half_pair(half, i):
-    return pl.ds(pl.multiple_of(half * (WIDE // 2) + i * LANES, LANES), LANES)
+    return pl.ds(pl.multiple_of(half * HALF_WIDE + i * LANES, LANES), LANES)
 
 
 def two_rows(value, rows):
@@ -94,55 +99,75 @@
     return copies
 
 
-def states_kernel(
-    x_hbm, b_hbm, c_hbm, log_hbm, grad_hbm,
-    send_ref, mine_ref, factor_ref,
-    x_ref, b_ref, c_ref, log_ref, grad_ref, sems,
+def states_of_half(
+    half, x_hbm, b_hbm, c_hbm, log_hbm, grad_hbm,
+    x_ref, b_ref, c_ref, log_ref, grad_ref, end_ref, start_ref, sems,
 ):
+    lanes = half_lanes(half)
     copies = load(
-        [(log_hbm, log_ref), (b_hbm, b_ref), (c_hbm, c_ref), (x_hbm, x_ref), (grad_hbm, grad_ref)],
+        [
+            (log_hbm, log_ref),
+            (b_hbm, b_ref),
+            (c_hbm, c_ref),
+            (x_hbm.at[:, lanes], x_ref),
+            (grad_hbm.at[:, lanes], grad_ref),
+        ],
         sems,
     )
     copies[0].wait()
-    cum = cumulative_columns(log_ref[...])
+    both = cumulative_columns(log_ref[...])
+    lower_half = jnp.full((TOK, HEADS // 2), half, jnp.int32) == 0
+    cum = jnp.where(lower_half, both[:, 0 : HEADS // 2], both[:, HEADS // 2 :])
     total = cum[TOK - 1 : TOK, :]
     to_end = jnp.exp(total - cum)
     from_start = jnp.exp(cum)
     last = jnp.exp(total)
+    for i in range(PAIRS // 2):
+        end_ref[:, pair(i)] = spread(to_end, i)
+        start_ref[:, pair(i)] = spread(from_start, i)
     copies[1].wait()
     b_t = transposed(b_ref[...])
     copies[2].wait()
     c_t = transposed(c_ref[...])
     copies[3].wait()
     copies[4].wait()
-    for g in range(PAIRS):
-        wx = (x_ref[:, pair(g)].astype(F32) * spread(to_end, g)).astype(BF16)
-        wg = (grad_ref[:, pair(g)].astype(F32) * spread(from_start, g)).astype(BF16)
-        ends = nn(b_t, wx)
-        opens = nn(c_t, wg)
-        factor = spread(last, g)
-        mine_ref[0:TOK, pair(g)] = ends
-        mine_ref[TOK : 2 * TOK, pair(g)] = opens
-        send_ref[0:TOK, pair(g)] = ends.astype(BF16)
-        send_ref[TOK : 2 * TOK, pair(g)] = opens.astype(BF16)
-        send_ref[2 * TOK : 2 * TOK + TAIL, pair(g)] = two_rows(factor, TAIL)
-        factor_ref[:, pair(g)] = jnp.broadcast_to(factor, (8, LANES))
-
-
-def chip_kernel(got_ref, mine_ref, factor_ref, send_ref):
-    half = core()
+    for i in range(PAIRS // 2):
+        wx = (x_ref[:, pair(i)].astype(F32) * end_ref[:, pair(i)]).astype(BF16)
+        wg = (grad_ref[:, pair(i)].astype(F32) * start_ref[:, pair(i)]).astype(BF16)
+        yield i, nn(b_t, wx), nn(c_t, wg), spread(last, i)
+
+
+def their_states_kernel(x_hbm, b_hbm, c_hbm, log_hbm, grad_hbm, send_ref, *scratch):
+    for i, ends, opens, factor in states_of_half(
+        1 - core(), x_hbm, b_hbm, c_hbm, log_hbm, grad_hbm, *scratch
+    ):
+        send_ref[0:TOK, pair(i)] = ends.astype(BF16)
+        send_ref[TOK : 2 * TOK, pair(i)] = opens.astype(BF16)
+        send_ref[2 * TOK : 2 * TOK + TAIL, pair(i)] = two_rows(factor, TAIL)
+
+
+def my_states_kernel(x_hbm, b_hbm, c_hbm, log_hbm, grad_hbm, mine_ref, factor_ref, *scratch):
+    for i, ends, opens, factor in states_of_half(
+        core(), x_hbm, b_hbm, c_hbm, log_hbm, grad_hbm, *scratch
+    ):
+        mine_ref[0:TOK, pair(i)] = ends
+        mine_ref[TOK : 2 * TOK, pair(i)] = opens
+        factor_ref[:, pair(i)] = jnp.broadcast_to(factor, (8, LANES))
+
+
+def chip_kernel(got_ref, mine_ref, factor_ref, send_hbm, send_ref, sems):
     first = first_core((TOK, LANES))
     first_row = first_core((1, LANES))
+    copies = []
     for i in range(PAIRS // 2):
-        lanes = half_pair(half, i)
-        mine = factor_ref[0:1, lanes]
-        theirs = one_row(got_ref[2 * TOK : 2 * TOK + TAIL, lanes])
+        mine = factor_ref[0:1, pair(i)]
+        theirs = one_row(got_ref[2 * TOK : 2 * TOK + TAIL, pair(i)])
         factor0 = jnp.where(first_row, mine, theirs)
         factor1 = jnp.where(first_row, theirs, mine)
-        my_ends = mine_ref[0:TOK, lanes]
-        my_opens = mine_ref[TOK : 2 * TOK, lanes]
-        ends = got_ref[0:TOK, lanes].astype(F32)
-        opens = got_ref[TOK : 2 * TOK, lanes].astype(F32)
+        my_ends = mine_ref[0:TOK, pair(i)]
+        my_opens = mine_ref[TOK : 2 * TOK, pair(i)]
+        ends = got_ref[0:TOK, pair(i)].astype(F32)
+        opens = got_ref[TOK : 2 * TOK, pair(i)].astype(F32)
         chip_ends = factor1 * jnp.where(first, my_ends, ends) + jnp.where(first, ends, my_ends)
         chip_opens = factor0 * jnp.where(first, opens, my_opens) + jnp.where(first, my_opens, opens)
         chip_ends = chip_ends.astype(BF16)
@@ -153,6 +178,11 @@
             send_ref[i * CHUNKS + r] = jnp.concatenate(
                 [chip_ends[rows], chip_opens[rows], factors], axis=0
             )
+        owners = pl.ds(i * CHUNKS, CHUNKS)
+        copies.append(pltpu.make_async_copy(send_ref.at[owners], send_hbm.at[owners], sems.at[i]))
+        copies[i].start()
+    for copy in copies:
+        copy.wait()
 
 
 def recurrence_kernel(got_ref, back_ref):
@@ -235,79 +265,78 @@
     return ref[i * CHUNKS : (i + 1) * CHUNKS, start : start + rows, :]
 
 
-def half_sums(half, back_ref, got_ref, wx_ref, wg_ref, b_sum, c_sum, state_ref):
-    first = first_core((TOK, LANES))
+def block_states(mine, back_ref, got_ref, mine_ref, factor_ref, out_ref):
+    inside_is_adjoint = first_core((TOK, LANES)) == mine
+    for i in range(PAIRS // 2):
+        my_factor = factor_ref[0:1, pair(i)]
+        their_factor = one_row(got_ref[2 * TOK : 2 * TOK + TAIL, pair(i)])
+        entry = slices(back_ref, i, 0, ROWS).reshape(TOK, LANES).astype(F32)
+        adjoint = slices(back_ref, i, ROWS, ROWS).reshape(TOK, LANES).astype(F32)
+        chip = one_row(jnp.sum(slices(back_ref, i, 2 * ROWS, 8).astype(F32), axis=0))
+        if mine:
+            opens = got_ref[TOK : 2 * TOK, pair(i)].astype(F32)
+            ends = got_ref[0:TOK, pair(i)].astype(F32)
+        else:
+            opens = mine_ref[TOK : 2 * TOK, pair(i)]
+            ends = mine_ref[0:TOK, pair(i)]
+        beyond, here, added = (
+            jnp.where(inside_is_adjoint, a, b)
+            for a, b in ((adjoint, entry), (entry, adjoint), (opens, ends))
+        )
+        factor, block_factor = (
+            (their_factor, my_factor) if mine else (my_factor, their_factor)
+        )
+        inside = factor * beyond + added
+        constant = block_factor * (factor * chip + jnp.sum(here * added, axis=0, keepdims=True))
+        out_ref[0:TOK, pair(i)] = jnp.where(inside_is_adjoint, here, inside).astype(BF16)
+        out_ref[TOK : 2 * TOK, pair(i)] = jnp.where(inside_is_adjoint, inside, here).astype(BF16)
+        out_ref[2 * TOK : 2 * TOK + TAIL, pair(i)] = two_rows(constant, TAIL)
+
+
+def half_sums(half, state_ref, wx_ref, wg_ref, b_sum, c_sum):
     for i in range(PAIRS // 2):
         lanes = half_pair(half, i)
-        theirs = one_row(got_ref[2 * TOK : 2 * TOK + TAIL, lanes])
-        entry = slices(back_ref, i, 0, ROWS).reshape(TOK, LANES)
-        adjoint = slices(back_ref, i, ROWS, ROWS).reshape(TOK, LANES)
-        inside = jnp.where(first, adjoint.astype(F32), entry.astype(F32)) * theirs
-        added = jnp.where(
-            first, got_ref[TOK : 2 * TOK, lanes].astype(F32), got_ref[0:TOK, lanes].astype(F32)
-        )
-        inside = inside + added
-        entry = jnp.where(first, entry.astype(F32), inside).astype(BF16)
-        adjoint = jnp.where(first, inside, adjoint.astype(F32)).astype(BF16)
-        state_ref[0, :, i * LANES : (i + 1) * LANES] = entry
-        state_ref[1, :, i * LANES : (i + 1) * LANES] = adjoint
-        b_sum = b_sum + nt(wx_ref[:, lanes], adjoint)
-        c_sum = c_sum + nt(wg_ref[:, lanes], entry)
+        b_sum = b_sum + nt(wx_ref[:, lanes], state_ref[TOK : 2 * TOK, pair(i)])
+        c_sum = c_sum + nt(wg_ref[:, lanes], state_ref[0:TOK, pair(i)])
     return b_sum, c_sum
 
 
-def own_kernel(back_ref, got_ref, wx_ref, wg_ref, bc_ref, state_ref, part_ref):
-    part_ref[0], part_ref[1] = half_sums(
-        core(), back_ref, got_ref, wx_ref, wg_ref, bc_ref[0], bc_ref[1], state_ref
-    )
-
-
-def other_kernel(back_ref, got_ref, wx_ref, wg_ref, part_ref, state_ref, send_ref):
-    b_sum, c_sum = half_sums(
-        1 - core(), back_ref, got_ref, wx_ref, wg_ref, part_ref[0], part_ref[1], state_ref
-    )
-    b_out = b_sum.astype(BF16)
-    c_out = c_sum.astype(BF16)
-    for z in range(send_ref.shape[0]):
-        send_ref[z, 0:TOK, :] = b_out
-        send_ref[z, TOK : 2 * TOK, :] = c_out
+def their_block_kernel(back_ref, got_ref, mine_ref, factor_ref, state_ref):
+    block_states(False, back_ref, got_ref, mine_ref, factor_ref, state_ref)
+
+
+def my_block_kernel(
+    back_ref, got_ref, mine_ref, factor_ref, wx_ref, wg_ref, bc_ref, state_ref, part_ref
+):
+    block_states(True, back_ref, got_ref, mine_ref, factor_ref, state_ref)
+    part_ref[0], part_ref[1] = half_sums(core(), state_ref, wx_ref, wg_ref, bc_ref[0], bc_ref[1])
+
+
+def sums_kernel(other_ref, wx_ref, wg_ref, part_ref, send_hbm, sum_ref, sems):
+    b_sum, c_sum = half_sums(1 - core(), other_ref, wx_ref, wg_ref, part_ref[0], part_ref[1])
+    sum_ref[0:TOK, :] = b_sum.astype(BF16)
+    sum_ref[TOK : 2 * TOK, :] = c_sum.astype(BF16)
+    copies = load([(sum_ref, send_hbm.at[z]) for z in range(send_hbm.shape[0])], sems)
+    for copy in copies:
+        copy.wait()
 
 
 def grads_kernel(
-    own_ref, other_ref, own_state_ref, other_state_ref, got_ref, factor_ref,
-    wx_ref, wg_ref, mats_ref, gx_ref, inner_ref, end_ref,
-    out_ref, decay_ref,
+    own_ref, other_ref, wx_ref, wg_ref, mats_ref, gx_ref, inner_ref, end_ref, out_ref, decay_ref
 ):
-    first = first_core((TOK, LANES))
     b_mat = mats_ref[0]
     c_mat = mats_ref[1]
     last = iota(0) == TOK - 1
     alphas = jnp.zeros((TOK, LANES), F32)
     betas = jnp.zeros((TOK, LANES), F32)
-    for half, back_ref, state_ref in (
-        (core(), own_ref, own_state_ref),
-        (1 - core(), other_ref, other_state_ref),
-    ):
+    for half, state_ref in ((core(), own_ref), (1 - core(), other_ref)):
         for i in range(PAIRS // 2):
             lanes = half_pair(half, i)
-            entry = state_ref[0, :, i * LANES : (i + 1) * LANES]
-            adjoint = state_ref[1, :, i * LANES : (i + 1) * LANES]
-            from_adjoint = nn(b_mat, adjoint)
+            from_adjoint = nn(b_mat, state_ref[TOK : 2 * TOK, pair(i)])
             out_ref[:, lanes] = (gx_ref[:, lanes] + end_ref[:, lanes] * from_adjoint).astype(BF16)
             beta = wx_ref[:, lanes].astype(F32) * from_adjoint
-            alpha = wg_ref[:, lanes].astype(F32) * nn(c_mat, entry)
-            chip = one_row(jnp.sum(slices(back_ref, i, 2 * ROWS, 8).astype(F32), axis=0))
-            outer = jnp.where(
-                first,
-                slices(back_ref, i, 0, ROWS).reshape(TOK, LANES).astype(F32)
-                * got_ref[TOK : 2 * TOK, lanes].astype(F32),
-                slices(back_ref, i, ROWS, ROWS).reshape(TOK, LANES).astype(F32)
-                * got_ref[0:TOK, lanes].astype(F32),
-            )
-            theirs = one_row(got_ref[2 * TOK : 2 * TOK + TAIL, lanes])
-            constant = factor_ref[0:1, lanes] * (
-                theirs * chip + jnp.sum(outer, axis=0, keepdims=True)
-            )
+            alpha = wg_ref[:, lanes].astype(F32) * nn(c_mat, state_ref[0:TOK, pair(i)])
+            constant = one_row(state_ref[2 * TOK : 2 * TOK + TAIL, pair(i)])
             alpha = alpha + jnp.where(last, constant, 0.0)
             head = 2 * (half * (PAIRS // 2) + i)
             pick = (iota(1) == head + iota(0) // HALF).astype(BF16)
@@ -329,11 +358,13 @@
 HBM_SPEC = pl.BlockSpec(memory_space=pltpu.HBM)
 
 
-def call(body, outs, micros, *args, from_hbm=False, scratch=()):
+def call(body, outs, micros, *args, from_hbm=False, to_hbm=False, scratch=()):
     more = {}
     if from_hbm:
         more["in_specs"] = [HBM_SPEC] * len(args)
         args = [pltpu.with_memory_space_constraint(a, pltpu.HBM) for a in args]
+    if to_hbm:
+        more["out_specs"] = [HBM_SPEC] * len(outs)
     return pl.pallas_call(
         body,
         out_shape=[jax.ShapeDtypeStruct(s, d) for s, d in outs],
@@ -353,25 +384,46 @@
     swap = [(i, i ^ 1) for i in range(seq)]
     same_core = [[2 * m + c for m in range(chips)] for c in range(2)]
     wide = (TOK, WIDE)
-    half_state = ((2, TOK, WIDE // 2), BF16)
-    loaded = (
-        pltpu.VMEM(wide, BF16),
-        pltpu.VMEM((TOK, LANES), BF16),
-        pltpu.VMEM((TOK, LANES), BF16),
-        pltpu.VMEM((HEADS, TOK), F32),
-        pltpu.VMEM(wide, BF16),
+    half = (TOK, HALF_WIDE)
+    states = (2 * TOK + TAIL, HALF_WIDE)
+    slices_shape = (chips, SEND_ROWS, LANES)
+
+    def loaded(shape):
+        return (
+            pltpu.VMEM(shape, BF16),
+            pltpu.VMEM((TOK, LANES), BF16),
+            pltpu.VMEM((TOK, LANES), BF16),
+            pltpu.VMEM((HEADS, TOK), F32),
+            pltpu.VMEM(shape, BF16),
+        )
+
+    for_states = loaded(half) + (
+        pltpu.VMEM(half, F32),
+        pltpu.VMEM(half, F32),
         pltpu.SemaphoreType.DMA((5,)),
     )
-    send, mine, factor = call(
-        states_kernel,
-        [((2 * TOK + TAIL, WIDE), BF16), ((2 * TOK, WIDE), F32), ((8, WIDE), F32)],
+    (send,) = call(
+        their_states_kernel, [(states, BF16)], 1, *inputs, from_hbm=True, scratch=for_states
+    )
+    got = lax.ppermute(send, "seq", swap)
+    mine, factor = call(
+        my_states_kernel,
+        [((2 * TOK, HALF_WIDE), F32), ((8, HALF_WIDE), F32)],
         1,
         *inputs,
         from_hbm=True,
-        scratch=loaded,
-    )
-    got = lax.ppermute(send, "seq", swap)
-    (send,) = call(chip_kernel, [((chips, SEND_ROWS, LANES), BF16)], 1, got, mine, factor)
+        scratch=for_states,
+    )
+    (send,) = call(
+        chip_kernel,
+        [(slices_shape, BF16)],
+        1,
+        got,
+        mine,
+        factor,
+        to_hbm=True,
+        scratch=(pltpu.VMEM(slices_shape, BF16), pltpu.SemaphoreType.DMA((PAIRS // 2,))),
+    )
     gathered = lax.all_to_all(send, "seq", 0, 0, tiled=True, axis_index_groups=same_core)
     local = call(
         intra_kernel,
@@ -387,26 +439,35 @@
         3,
         *inputs,
         from_hbm=True,
-        scratch=loaded,
+        scratch=loaded(wide) + (pltpu.SemaphoreType.DMA((5,)),),
     )
     gathered, (gx, inner, bc, wx, wg, mats, end) = lax.optimization_barrier((gathered, local))
-    (back,) = call(recurrence_kernel, [((chips, SEND_ROWS, LANES), BF16)], 1, gathered)
+    (back,) = call(recurrence_kernel, [(slices_shape, BF16)], 1, gathered)
     back = lax.all_to_all(back, "seq", 0, 0, tiled=True, axis_index_groups=same_core)
-    other = lax.ppermute(back, "seq", swap)
-    own_state, part = call(
-        own_kernel, [half_state, ((2, TOK, LANES), F32)], 1, back, got, wx, wg, bc
-    )
-    other_state, parts = call(
-        other_kernel,
-        [half_state, ((heads, 2 * TOK, LANES), BF16)],
-        1, other, got, wx, wg, part,
+    (send,) = call(their_block_kernel, [(states, BF16)], 1, back, got, mine, factor)
+    other = lax.ppermute(send, "seq", swap)
+    own, part = call(
+        my_block_kernel,
+        [(states, BF16), ((2, TOK, LANES), F32)],
+        1, back, got, mine, factor, wx, wg, bc,
+    )
+    (parts,) = call(
+        sums_kernel,
+        [((heads, 2 * TOK, LANES), BF16)],
+        1,
+        other,
+        wx,
+        wg,
+        part,
+        to_hbm=True,
+        scratch=(pltpu.VMEM((2 * TOK, LANES), BF16), pltpu.SemaphoreType.DMA((heads,))),
     )
     parts = lax.all_to_all(parts, "head", 0, 0, tiled=True)
     grad_x, decay_grad = call(
         grads_kernel,
         [(wide, BF16), ((HEADS, TOK), F32)],
         3,
-        back, other, own_state, other_state, got, factor, wx, wg, mats, gx, inner, end,
+        own, other, wx, wg, mats, gx, inner, end,
     )
     parts, grad_x, decay_grad = lax.optimization_barrier((parts, grad_x, decay_grad))
     grad_b, grad_c = call(head_sum_kernel, [((TOK, LANES), BF16)] * 2, 1, parts)

time: 84 us -> 84.5 us (level)
  local copies, waits for them, and re-layouts: 1.83 us -> 0 us
  Pallas kernels: 10.8 us -> 12.6 us
  waiting for transfers between devices: 23.5 us -> 24.6 us
    unnamed x4 -> x0, local copies, waits for them, and re-layouts: 1.83 us -> none
    pallas_call x8 -> x10, Pallas kernels: 10.8 us -> 12.6 us  [call(): pl.pallas_call(body, out_shape=[jax.ShapeDtypeStruct(s, d) for s, d in ou...]
    all_to_all x1, waiting for transfers between devices: 6.5 us -> 8.15 us  [per_device(): lax.all_to_all(send, 'seq', 0, 0, tiled=True, axis_index_groups=same_core)]
    ppermute x1, waiting for transfers between devices: 1.56 us -> 0.01 us  [per_device(): got = lax.ppermute(send, 'seq', swap)]
    all_to_all x1, waiting for transfers between devices: 14.6 us -> 15.6 us  [per_device(): parts = lax.all_to_all(parts, 'head', 0, 0, tiled=True)]
  transfers between devices with their start and end apart: 4 -> 4, of which waited for: 4 -> 3; matrix products, arithmetic and copies ran while one was open for 0% -> 0% of each run, Pallas kernels for 7% -> 9%
where the time goes in v3:
time: 84.5 us; the launch traced here: 84 us
  starting transfers between devices  29.4 us (35%)
  waiting for transfers between devices  24.6 us (29%)
  blocking collectives  16.7 us (20%)
  Pallas kernels  12.6 us (15%)
    all_to_all x1, blocking collectives, per_device(): lax.all_to_all(back, 'seq', 0, 0, tiled=True, axis_index_groups=same_core)  16.7 us
    all_to_all x1, waiting for transfers between devices, per_device(): parts = lax.all_to_all(parts, 'head', 0, 0, tiled=True)  15.6 us
    pallas_call x10, Pallas kernels, call(): pl.pallas_call(body, out_shape=[jax.ShapeDtypeStruct(s, d) for s, d in ou...  12.6 us
    all_to_all x1, starting transfers between devices, per_device(): parts = lax.all_to_all(parts, 'head', 0, 0, tiled=True)  10 us
    ppermute x1, starting transfers between devices, per_device(): got = lax.ppermute(send, 'seq', swap)  8.79 us
    all_to_all x1, waiting for transfers between devices, per_device(): lax.all_to_all(send, 'seq', 0, 0, tiled=True, axis_index_groups=same_core)  8.15 us
    ppermute x1, starting transfers between devices, per_device(): other = lax.ppermute(send, 'seq', swap)  6.28 us
    all_to_all x1, starting transfers between devices, per_device(): lax.all_to_all(send, 'seq', 0, 0, tiled=True, axis_index_groups=same_core)  4.31 us
  transfers between devices with their start and end apart: 4, of which 3 were waited for; matrix products, arithmetic and copies ran while one was open for 0% of the time, Pallas kernels for 9%

profile of v3, /device:TPU:1, one launch (start us, length us, event | category | flops | bytes accessed | tf_op | source)
XLA Modules:
  0.0 84.0 jit_solution(18426005135584198600)
XLA Ops:
  0.6 1.9 %shard_map.84 = bf16[272,512]{1,0:T(8,128)(2,1)S(1)} custom-call(bf16[128,1024]{1,0:T(8,128)(2,1)} %x_hbm.5, bf16[128,128]{1,0:T(8,128)(2,1)} %b_hbm.5, bf16[128,128]{1,0:T(8,128)(2,1)} %c_hbm.5, f32[16,128]{1,0:T(8,128)} %log_hbm.5, bf16[128,1024]{1,0:T(8,128)(2,1)} %grad_hbm.5), custom_call_target="tpu_custom_call" | custom-call | flops 1000000000 | bytes 262144 | tf_op jit(solution)/shard_map/pallas_call | solution.py:368
  2.5 8.8 %collective-permute-start = (bf16[272,512]{1,0:T(8,128)(2,1)S(1)}, bf16[272,512]{1,0:T(8,128)(2,1)S(1)}, u32[]{:S(2)}, u32[]{:S(2)}) collective-permute-start(bf16[272,512]{1,0:T(8,128)(2,1)S(1)} %shard_map.84), channel_id=1, source_target_pairs={{0,8},{8,0},{16,24},{24,16},{32,40},{40,32},{48,56},{56,48},{64,72... | collective-permute-start | bytes 835592 | tf_op jit(solution)/shard_map/ppermute | solution.py:408
  11.3 1.9 %shard_map.85 = (f32[256,512]{1,0:T(8,128)S(1)}, f32[8,512]{1,0:T(8,128)S(1)}) custom-call(bf16[128,1024]{1,0:T(8,128)(2,1)} %x_hbm.5, bf16[128,128]{1,0:T(8,128)(2,1)} %b_hbm.5, bf16[128,128]{1,0:T(8,128)(2,1)} %c_hbm.5, f32[16,128]{1,0:T(8,128)} %log_hbm.5, bf16[128,1024]{1,0:T(8,128)(2,1)} %grad_hbm.5), custom_call_target="tpu_custom_call" | custom-call | flops 1000000000 | bytes 262144 | tf_op jit(solution)/shard_map/pallas_call | solution.py:368
  13.2 0.0 collective-permute-done.got_ref
  13.2 0.8 shard_map.86
  14.0 4.3 %all-to-all-start = ((bf16[32,40,128]{2,1,0:T(8,128)(2,1)}), bf16[32,40,128]{2,1,0:T(8,128)(2,1)S(1)}, u32[]{:S(2)}, u32[]{:S(2)}) async-start(bf16[32,40,128]{2,1,0:T(8,128)(2,1)} %shard_map.86), calls=%async_computation | async-start | bytes 655360 | tf_op jit(solution)/shard_map/all_to_all | solution.py:427
  18.4 3.2 %shard_map.87 = (f32[128,1024]{1,0:T(8,128)S(1)}, f32[16,128]{1,0:T(8,128)S(1)}, f32[2,128,128]{2,1,0:T(8,128)S(1)}, bf16[128,1024]{1,0:T(8,128)(2,1)S(1)}, bf16...) custom-call(bf16[128,1024]{1,0:T(8,128)(2,1)} %x_hbm.5, ...), custom_call_target="tpu_custom_call" | custom-call | flops 3000000000 | bytes 262144 | tf_op jit(solution)/shard_map/pallas_call | solution.py:368
  21.5 8.2 %all-to-all-done.got_ref = bf16[32,40,128]{2,1,0:T(8,128)(2,1)S(1)} async-done(((bf16[32,40,128]{2,1,0:T(8,128)(2,1)}), bf16[32,40,128]{2,1,0:T(8,128)(2,1)S(1)}, u32[]{:S(2)}, u32[]{:S(2)}) %all-to-all-start) | async-done | bytes 327712 | tf_op jit(solution)/shard_map/all_to_all | solution.py:427
  29.7 0.2 shard_map.88
  29.8 16.7 %all_to_all.15.back_ref = bf16[32,40,128]{2,1,0:T(8,128)(2,1)S(1)} all-to-all(bf16[32,40,128]{2,1,0:T(8,128)(2,1)S(1)} %shard_map.88), channel_id=1, replica_groups={{0,16,32,48,64,80,96,112,128,144,160,176,192,208,224,240,256,272,288,30..., dimensions={0} | all-to-all | bytes 655360 | tf_op jit(solution)/shard_map/all_to_all | solution.py:446
  46.5 0.1 shard_map.89
  46.7 6.3 %collective-permute-start.1 = (bf16[272,512]{1,0:T(8,128)(2,1)S(1)}, bf16[272,512]{1,0:T(8,128)(2,1)S(1)}, u32[]{:S(2)}, u32[]{:S(2)}) collective-permute-start(bf16[272,512]{1,0:T(8,128)(2,1)S(1)} %shard_map.89), channel_id=1, source_target_pairs={{0,8},{8,0},{16,24},{24,16},{32,40},{40,32},{48,56},{56,48},{64,72... | collective-permute-start | bytes 835592 | tf_op jit(solution)/shard_map/ppermute | solution.py:448
  52.9 0.3 shard_map.90
  53.3 0.8 collective-permute-done.1.other_ref
  54.1 1.2 %shard_map.91 = bf16[8,256,128]{2,1,0:T(8,128)(2,1)} custom-call(bf16[272,512]{1,0:T(8,128)(2,1)S(1)} %collective-permute-done.1.other_ref, bf16[128,1024]{1,0:T(8,128)(2,1)S(1)} %get-tuple-element.40.wx_ref, bf16[128,1024]{1,0:T(8,128)(2,1)S(1)} %get-tuple-element.41.wg_ref, f32[2,128,128]{2,1,0:T(8,128)S(1)} %get-tuple-element.43.part_ref), custom_call_target="tpu_custom_call" | custom-call | flops 1000000000 | bytes 262144 | tf_op jit(solution)/shard_map/pallas_call | solution.py:368
  55.3 10.0 %all-to-all-start.2 = ((bf16[8,256,128]{2,1,0:T(8,128)(2,1)}), bf16[8,256,128]{2,1,0:T(8,128)(2,1)S(1)}, u32[]{:S(2)}, u32[]{:S(2)}) async-start(bf16[8,256,128]{2,1,0:T(8,128)(2,1)} %shard_map.91), calls=%async_computation.2 | async-start | bytes 1048576 | tf_op jit(solution)/shard_map/all_to_all | solution.py:465
  65.3 2.3 %shard_map.92 = (bf16[128,1024]{1,0:T(8,128)(2,1)}, f32[16,128]{1,0:T(8,128)}) custom-call(bf16[272,512]{1,0:T(8,128)(2,1)S(1)} %get-tuple-element.44.own_ref, bf16[272,512]{1,0:T(8,128)(2,1)S(1)} %collective-permute-done.1.other_ref, bf16[128,1024]{1,0:T(8,128)(2,1)S(1)} %get-tuple-element.40.wx_ref, bf16[128,1024]{1,0:T(8,128)(2,1)S(1)} %get-tuple-element.41.wg_ref, ...), custom_call_target="tpu_custom_call" | custom-call | flops 3000000000 | bytes 262144 | tf_op jit(solution)/shard_map/pallas_call | solution.py:368
  67.7 15.6 %all-to-all-done.2.parts_ref = bf16[8,256,128]{2,1,0:T(8,128)(2,1)S(1)} async-done(((bf16[8,256,128]{2,1,0:T(8,128)(2,1)}), bf16[8,256,128]{2,1,0:T(8,128)(2,1)S(1)}, u32[]{:S(2)}, u32[]{:S(2)}) %all-to-all-start.2) | async-done | bytes 524320 | tf_op jit(solution)/shard_map/all_to_all | solution.py:465
  83.3 0.7 shard_map.93
Async XLA Ops:
  2.5 10.7 %collective-permute-start = (bf16[272,512]{1,0:T(8,128)(2,1)S(1)}, bf16[272,512]{1,0:T(8,128)(2,1)S(1)}, u32[]{:S(2)}, u32[]{:S(2)}) collective-permute-start(bf16[272,512]{1,0:T(8,128)(2,1)S(1)} %shard_map.84), channel_id=1, source_target_pairs={{0,8},{8,0},{16,24},{24,16},{32,40},{40,32},{48,56},{56,48},{64,72... | collective-permute-start | bytes 835592 | tf_op jit(solution)/shard_map/ppermute | solution.py:408
  14.0 15.6 %all-to-all-start = ((bf16[32,40,128]{2,1,0:T(8,128)(2,1)}), bf16[32,40,128]{2,1,0:T(8,128)(2,1)S(1)}, u32[]{:S(2)}, u32[]{:S(2)}) async-start(bf16[32,40,128]{2,1,0:T(8,128)(2,1)} %shard_map.86), calls=%async_computation | async-start | bytes 655360 | tf_op jit(solution)/shard_map/all_to_all | solution.py:427
  46.7 7.4 %collective-permute-start.1 = (bf16[272,512]{1,0:T(8,128)(2,1)S(1)}, bf16[272,512]{1,0:T(8,128)(2,1)S(1)}, u32[]{:S(2)}, u32[]{:S(2)}) collective-permute-start(bf16[272,512]{1,0:T(8,128)(2,1)S(1)} %shard_map.89), channel_id=1, source_target_pairs={{0,8},{8,0},{16,24},{24,16},{32,40},{40,32},{48,56},{56,48},{64,72... | collective-permute-start | bytes 835592 | tf_op jit(solution)/shard_map/ppermute | solution.py:448
  55.3 28.0 %all-to-all-start.2 = ((bf16[8,256,128]{2,1,0:T(8,128)(2,1)}), bf16[8,256,128]{2,1,0:T(8,128)(2,1)S(1)}, u32[]{:S(2)}, u32[]{:S(2)}) async-start(bf16[8,256,128]{2,1,0:T(8,128)(2,1)} %shard_map.91), calls=%async_computation.2 | async-start | bytes 1048576 | tf_op jit(solution)/shard_map/all_to_all | solution.py:465

commit v4 on v3

--- a/solution.py
+++ b/solution.py
@@ -99,25 +99,7 @@
     return copies
 
 
-def states_of_half(
-    half, x_hbm, b_hbm, c_hbm, log_hbm, grad_hbm,
-    x_ref, b_ref, c_ref, log_ref, grad_ref, end_ref, start_ref, sems,
-):
-    lanes = half_lanes(half)
-    copies = load(
-        [
-            (log_hbm, log_ref),
-            (b_hbm, b_ref),
-            (c_hbm, c_ref),
-            (x_hbm.at[:, lanes], x_ref),
-            (grad_hbm.at[:, lanes], grad_ref),
-        ],
-        sems,
-    )
-    copies[0].wait()
-    both = cumulative_columns(log_ref[...])
-    lower_half = jnp.full((TOK, HEADS // 2), half, jnp.int32) == 0
-    cum = jnp.where(lower_half, both[:, 0 : HEADS // 2], both[:, HEADS // 2 :])
+def states_of_half(cum, b_t, c_t, x_ref, grad_ref, end_ref, start_ref, copies=()):
     total = cum[TOK - 1 : TOK, :]
     to_end = jnp.exp(total - cum)
     from_start = jnp.exp(cum)
@@ -125,30 +107,60 @@
     for i in range(PAIRS // 2):
         end_ref[:, pair(i)] = spread(to_end, i)
         start_ref[:, pair(i)] = spread(from_start, i)
-    copies[1].wait()
-    b_t = transposed(b_ref[...])
-    copies[2].wait()
-    c_t = transposed(c_ref[...])
-    copies[3].wait()
-    copies[4].wait()
+    for copy in copies:
+        copy.wait()
     for i in range(PAIRS // 2):
         wx = (x_ref[:, pair(i)].astype(F32) * end_ref[:, pair(i)]).astype(BF16)
         wg = (grad_ref[:, pair(i)].astype(F32) * start_ref[:, pair(i)]).astype(BF16)
         yield i, nn(b_t, wx), nn(c_t, wg), spread(last, i)
 
 
-def their_states_kernel(x_hbm, b_hbm, c_hbm, log_hbm, grad_hbm, send_ref, *scratch):
+def their_states_kernel(
+    x_hbm, b_hbm, c_hbm, log_hbm, grad_hbm,
+    send_ref, x_mine, grad_mine, cum_mine, b_t_ref, c_t_ref,
+    x_ref, b_ref, c_ref, log_ref, grad_ref, end_ref, start_ref, sems,
+):
+    theirs = half_lanes(1 - core())
+    mine = half_lanes(core())
+    copies = load(
+        [
+            (log_hbm, log_ref),
+            (b_hbm, b_ref),
+            (c_hbm, c_ref),
+            (x_hbm.at[:, theirs], x_ref),
+            (grad_hbm.at[:, theirs], grad_ref),
+            (x_hbm.at[:, mine], x_mine),
+            (grad_hbm.at[:, mine], grad_mine),
+        ],
+        sems,
+    )
+    copies[0].wait()
+    both = cumulative_columns(log_ref[...])
+    lower, upper = both[:, 0 : HEADS // 2], both[:, HEADS // 2 :]
+    lower_mine = first_core((TOK, HEADS // 2))
+    cum_mine[...] = jnp.where(lower_mine, lower, upper)
+    copies[1].wait()
+    b_t = transposed(b_ref[...])
+    b_t_ref[...] = b_t
+    copies[2].wait()
+    c_t = transposed(c_ref[...])
+    c_t_ref[...] = c_t
     for i, ends, opens, factor in states_of_half(
-        1 - core(), x_hbm, b_hbm, c_hbm, log_hbm, grad_hbm, *scratch
+        jnp.where(lower_mine, upper, lower),
+        b_t, c_t, x_ref, grad_ref, end_ref, start_ref, copies[3:5],
     ):
         send_ref[0:TOK, pair(i)] = ends.astype(BF16)
         send_ref[TOK : 2 * TOK, pair(i)] = opens.astype(BF16)
         send_ref[2 * TOK : 2 * TOK + TAIL, pair(i)] = two_rows(factor, TAIL)
-
-
-def my_states_kernel(x_hbm, b_hbm, c_hbm, log_hbm, grad_hbm, mine_ref, factor_ref, *scratch):
+    copies[5].wait()
+    copies[6].wait()
+
+
+def my_states_kernel(
+    x_ref, grad_ref, cum_ref, b_t_ref, c_t_ref, mine_ref, factor_ref, end_ref, start_ref
+):
     for i, ends, opens, factor in states_of_half(
-        core(), x_hbm, b_hbm, c_hbm, log_hbm, grad_hbm, *scratch
+        cum_ref[...], b_t_ref[...], c_t_ref[...], x_ref, grad_ref, end_ref, start_ref
     ):
         mine_ref[0:TOK, pair(i)] = ends
         mine_ref[TOK : 2 * TOK, pair(i)] = opens
@@ -293,12 +305,10 @@
         out_ref[2 * TOK : 2 * TOK + TAIL, pair(i)] = two_rows(constant, TAIL)
 
 
-def half_sums(half, state_ref, wx_ref, wg_ref, b_sum, c_sum):
+def half_sum(half, state_ref, weighted_ref, start, total):
     for i in range(PAIRS // 2):
-        lanes = half_pair(half, i)
-        b_sum = b_sum + nt(wx_ref[:, lanes], state_ref[TOK : 2 * TOK, pair(i)])
-        c_sum = c_sum + nt(wg_ref[:, lanes], state_ref[0:TOK, pair(i)])
-    return b_sum, c_sum
+        total = total + nt(weighted_ref[:, half_pair(half, i)], state_ref[start : start + TOK, pair(i)])
+    return total
 
 
 def their_block_kernel(back_ref, got_ref, mine_ref, factor_ref, state_ref):
@@ -309,14 +319,20 @@
     back_ref, got_ref, mine_ref, factor_ref, wx_ref, wg_ref, bc_ref, state_ref, part_ref
 ):
     block_states(True, back_ref, got_ref, mine_ref, factor_ref, state_ref)
-    part_ref[0], part_ref[1] = half_sums(core(), state_ref, wx_ref, wg_ref, bc_ref[0], bc_ref[1])
+    part_ref[0] = half_sum(core(), state_ref, wx_ref, TOK, bc_ref[0])
+    part_ref[1] = half_sum(core(), state_ref, wg_ref, 0, bc_ref[1])
 
 
 def sums_kernel(other_ref, wx_ref, wg_ref, part_ref, send_hbm, sum_ref, sems):
-    b_sum, c_sum = half_sums(1 - core(), other_ref, wx_ref, wg_ref, part_ref[0], part_ref[1])
-    sum_ref[0:TOK, :] = b_sum.astype(BF16)
-    sum_ref[TOK : 2 * TOK, :] = c_sum.astype(BF16)
-    copies = load([(sum_ref, send_hbm.at[z]) for z in range(send_hbm.shape[0])], sems)
+    count = send_hbm.shape[0]
+    copies = []
+    for k, (weighted_ref, start) in enumerate(((wx_ref, TOK), (wg_ref, 0))):
+        total = half_sum(1 - core(), other_ref, weighted_ref, start, part_ref[k])
+        rows = pl.ds(k * TOK, TOK)
+        sum_ref[rows, :] = total.astype(BF16)
+        copies += load(
+            [(sum_ref.at[rows], send_hbm.at[z, rows]) for z in range(count)], sems.at[k]
+        )
     for copy in copies:
         copy.wait()
 
@@ -397,22 +413,23 @@
             pltpu.VMEM(shape, BF16),
         )
 
-    for_states = loaded(half) + (
-        pltpu.VMEM(half, F32),
-        pltpu.VMEM(half, F32),
-        pltpu.SemaphoreType.DMA((5,)),
-    )
-    (send,) = call(
-        their_states_kernel, [(states, BF16)], 1, *inputs, from_hbm=True, scratch=for_states
+    spreads = (pltpu.VMEM(half, F32), pltpu.VMEM(half, F32))
+    square = ((TOK, LANES), BF16)
+    send, *for_mine = call(
+        their_states_kernel,
+        [(states, BF16), (half, BF16), (half, BF16), ((TOK, HEADS // 2), F32), square, square],
+        1,
+        *inputs,
+        from_hbm=True,
+        scratch=loaded(half) + spreads + (pltpu.SemaphoreType.DMA((7,)),),
     )
     got = lax.ppermute(send, "seq", swap)
     mine, factor = call(
         my_states_kernel,
         [((2 * TOK, HALF_WIDE), F32), ((8, HALF_WIDE), F32)],
         1,
-        *inputs,
-        from_hbm=True,
-        scratch=for_states,
+        *for_mine,
+        scratch=spreads,
     )
     (send,) = call(
         chip_kernel,
@@ -460,7 +477,7 @@
         wg,
         part,
         to_hbm=True,
-        scratch=(pltpu.VMEM((2 * TOK, LANES), BF16), pltpu.SemaphoreType.DMA((heads,))),
+        scratch=(pltpu.VMEM((2 * TOK, LANES), BF16), pltpu.SemaphoreType.DMA((2, heads))),
     )
     parts = lax.all_to_all(parts, "head", 0, 0, tiled=True)
     grad_x, decay_grad = call(

time: 84.5 us -> 83.6 us (0.989)
  Pallas kernels: 12.6 us -> 11.3 us
    pallas_call x10, Pallas kernels: 12.6 us -> 11.3 us  [call(): pl.pallas_call(body, out_shape=[jax.ShapeDtypeStruct(s, d) for s, d in ou...]
    all_to_all x1, waiting for transfers between devices: 8.15 us -> 7.3 us  [per_device(): lax.all_to_all(send, 'seq', 0, 0, tiled=True, axis_index_groups=same_core)]
  transfers between devices with their start and end apart: 4 -> 4, of which waited for: 3 -> 4; matrix products, arithmetic and copies ran while one was open for 0% -> 0% of each run, Pallas kernels for 9% -> 8%
where the time goes in v4:
time: 83.6 us; the launch traced here: 83.1 us
  starting transfers between devices  29.5 us (35%)
  waiting for transfers between devices  24.3 us (29%)
  blocking collectives  17.3 us (21%)
  Pallas kernels  11.3 us (14%)
    all_to_all x1, blocking collectives, per_device(): lax.all_to_all(back, 'seq', 0, 0, tiled=True, axis_index_groups=same_core)  17.3 us
    all_to_all x1, waiting for transfers between devices, per_device(): parts = lax.all_to_all(parts, 'head', 0, 0, tiled=True)  15.6 us
    pallas_call x10, Pallas kernels, call(): pl.pallas_call(body, out_shape=[jax.ShapeDtypeStruct(s, d) for s, d in ou...  11.3 us
    all_to_all x1, starting transfers between devices, per_device(): parts = lax.all_to_all(parts, 'head', 0, 0, tiled=True)  10 us
    ppermute x1, starting transfers between devices, per_device(): got = lax.ppermute(send, 'seq', swap)  8.79 us
    all_to_all x1, waiting for transfers between devices, per_device(): lax.all_to_all(send, 'seq', 0, 0, tiled=True, axis_index_groups=same_core)  7.3 us
    ppermute x1, starting transfers between devices, per_device(): other = lax.ppermute(send, 'seq', swap)  6.37 us
    all_to_all x1, starting transfers between devices, per_device(): lax.all_to_all(send, 'seq', 0, 0, tiled=True, axis_index_groups=same_core)  4.31 us
  transfers between devices with their start and end apart: 4, of which 4 were waited for; matrix products, arithmetic and copies ran while one was open for 0% of the time, Pallas kernels for 8%

profile of v4, /device:TPU:1, one launch (start us, length us, event | category | flops | bytes accessed | tf_op | source)
XLA Modules:
  0.0 83.1 jit_solution(1033244495772171396)
XLA Ops:
  0.6 1.9 %shard_map.84 = (bf16[272,512]{1,0:T(8,128)(2,1)S(1)}, bf16[128,512]{1,0:T(8,128)(2,1)S(1)}, bf16[128,512]{1,0:T(8,128)(2,1)S(1)}, f32[128,8]{1,0:T(8,128)S(1)},...) custom-call(bf16[128,1024]{1,0:T(8,128)(2,1)} %x_hbm.3, bf16[128,128]{1,0:T(8,128)(2,1)} %b_hbm.3, ...), custom_call_target="tpu_custom_call" | custom-call | flops 1000000000 | bytes 262144 | tf_op jit(solution)/shard_map/pallas_call | solution.py:384
  2.5 8.8 %collective-permute-start = (bf16[272,512]{1,0:T(8,128)(2,1)S(1)}, bf16[272,512]{1,0:T(8,128)(2,1)S(1)}, u32[]{:S(2)}, u32[]{:S(2)}) collective-permute-start(bf16[272,512]{1,0:T(8,128)(2,1)S(1)} %get-tuple-element.36), channel_id=1, source_target_pairs={{0,8},{8,0},{16,24},{24,16},{32,40},{40,32},{48,56},{56,48},{64,72... | collective-permute-start | bytes 835592 | tf_op jit(solution)/shard_map/ppermute | solution.py:426
  11.3 0.6 shard_map.85
  11.9 0.6 collective-permute-done.got_ref
  12.5 0.8 shard_map.86
  13.3 4.3 %all-to-all-start = ((bf16[32,40,128]{2,1,0:T(8,128)(2,1)}), bf16[32,40,128]{2,1,0:T(8,128)(2,1)S(1)}, u32[]{:S(2)}, u32[]{:S(2)}) async-start(bf16[32,40,128]{2,1,0:T(8,128)(2,1)} %shard_map.86), calls=%async_computation | async-start | bytes 655360 | tf_op jit(solution)/shard_map/all_to_all | solution.py:444
  17.6 3.2 %shard_map.87 = (f32[128,1024]{1,0:T(8,128)S(1)}, f32[16,128]{1,0:T(8,128)S(1)}, f32[2,128,128]{2,1,0:T(8,128)S(1)}, bf16[128,1024]{1,0:T(8,128)(2,1)S(1)}, bf16...) custom-call(bf16[128,1024]{1,0:T(8,128)(2,1)} %x_hbm.3, ...), custom_call_target="tpu_custom_call" | custom-call | flops 3000000000 | bytes 262144 | tf_op jit(solution)/shard_map/pallas_call | solution.py:384
  20.8 7.3 %all-to-all-done.got_ref = bf16[32,40,128]{2,1,0:T(8,128)(2,1)S(1)} async-done(((bf16[32,40,128]{2,1,0:T(8,128)(2,1)}), bf16[32,40,128]{2,1,0:T(8,128)(2,1)S(1)}, u32[]{:S(2)}, u32[]{:S(2)}) %all-to-all-start) | async-done | bytes 327712 | tf_op jit(solution)/shard_map/all_to_all | solution.py:444
  28.1 0.2 shard_map.88
  28.2 17.3 %all_to_all.15.back_ref = bf16[32,40,128]{2,1,0:T(8,128)(2,1)S(1)} all-to-all(bf16[32,40,128]{2,1,0:T(8,128)(2,1)S(1)} %shard_map.88), channel_id=1, replica_groups={{0,16,32,48,64,80,96,112,128,144,160,176,192,208,224,240,256,272,288,30..., dimensions={0} | all-to-all | bytes 655360 | tf_op jit(solution)/shard_map/all_to_all | solution.py:463
  45.5 0.1 shard_map.89
  45.7 6.4 %collective-permute-start.1 = (bf16[272,512]{1,0:T(8,128)(2,1)S(1)}, bf16[272,512]{1,0:T(8,128)(2,1)S(1)}, u32[]{:S(2)}, u32[]{:S(2)}) collective-permute-start(bf16[272,512]{1,0:T(8,128)(2,1)S(1)} %shard_map.89), channel_id=1, source_target_pairs={{0,8},{8,0},{16,24},{24,16},{32,40},{40,32},{48,56},{56,48},{64,72... | collective-permute-start | bytes 835592 | tf_op jit(solution)/shard_map/ppermute | solution.py:465
  52.0 0.4 shard_map.90
  52.4 0.8 collective-permute-done.1.other_ref
  53.2 1.2 %shard_map.91 = bf16[8,256,128]{2,1,0:T(8,128)(2,1)} custom-call(bf16[272,512]{1,0:T(8,128)(2,1)S(1)} %collective-permute-done.1.other_ref, bf16[128,1024]{1,0:T(8,128)(2,1)S(1)} %get-tuple-element.52.wx_ref, bf16[128,1024]{1,0:T(8,128)(2,1)S(1)} %get-tuple-element.53.wg_ref, f32[2,128,128]{2,1,0:T(8,128)S(1)} %get-tuple-element.55.part_ref), custom_call_target="tpu_custom_call" | custom-call | flops 1000000000 | bytes 262144 | tf_op jit(solution)/shard_map/pallas_call | solution.py:384
  54.5 10.0 %all-to-all-start.2 = ((bf16[8,256,128]{2,1,0:T(8,128)(2,1)}), bf16[8,256,128]{2,1,0:T(8,128)(2,1)S(1)}, u32[]{:S(2)}, u32[]{:S(2)}) async-start(bf16[8,256,128]{2,1,0:T(8,128)(2,1)} %shard_map.91), calls=%async_computation.2 | async-start | bytes 1048576 | tf_op jit(solution)/shard_map/all_to_all | solution.py:482
  64.5 2.3 %shard_map.92 = (bf16[128,1024]{1,0:T(8,128)(2,1)}, f32[16,128]{1,0:T(8,128)}) custom-call(bf16[272,512]{1,0:T(8,128)(2,1)S(1)} %get-tuple-element.56.own_ref, bf16[272,512]{1,0:T(8,128)(2,1)S(1)} %collective-permute-done.1.other_ref, bf16[128,1024]{1,0:T(8,128)(2,1)S(1)} %get-tuple-element.52.wx_ref, bf16[128,1024]{1,0:T(8,128)(2,1)S(1)} %get-tuple-element.53.wg_ref, ...), custom_call_target="tpu_custom_call" | custom-call | flops 3000000000 | bytes 262144 | tf_op jit(solution)/shard_map/pallas_call | solution.py:384
  66.9 15.6 %all-to-all-done.2.parts_ref = bf16[8,256,128]{2,1,0:T(8,128)(2,1)S(1)} async-done(((bf16[8,256,128]{2,1,0:T(8,128)(2,1)}), bf16[8,256,128]{2,1,0:T(8,128)(2,1)S(1)}, u32[]{:S(2)}, u32[]{:S(2)}) %all-to-all-start.2) | async-done | bytes 524320 | tf_op jit(solution)/shard_map/all_to_all | solution.py:482
  82.5 0.7 shard_map.93
Async XLA Ops:
  2.5 10.0 %collective-permute-start = (bf16[272,512]{1,0:T(8,128)(2,1)S(1)}, bf16[272,512]{1,0:T(8,128)(2,1)S(1)}, u32[]{:S(2)}, u32[]{:S(2)}) collective-permute-start(bf16[272,512]{1,0:T(8,128)(2,1)S(1)} %get-tuple-element.36), channel_id=1, source_target_pairs={{0,8},{8,0},{16,24},{24,16},{32,40},{40,32},{48,56},{56,48},{64,72... | collective-permute-start | bytes 835592 | tf_op jit(solution)/shard_map/ppermute | solution.py:426
  13.3 14.8 %all-to-all-start = ((bf16[32,40,128]{2,1,0:T(8,128)(2,1)}), bf16[32,40,128]{2,1,0:T(8,128)(2,1)S(1)}, u32[]{:S(2)}, u32[]{:S(2)}) async-start(bf16[32,40,128]{2,1,0:T(8,128)(2,1)} %shard_map.86), calls=%async_computation | async-start | bytes 655360 | tf_op jit(solution)/shard_map/all_to_all | solution.py:444
  45.7 7.5 %collective-permute-start.1 = (bf16[272,512]{1,0:T(8,128)(2,1)S(1)}, bf16[272,512]{1,0:T(8,128)(2,1)S(1)}, u32[]{:S(2)}, u32[]{:S(2)}) collective-permute-start(bf16[272,512]{1,0:T(8,128)(2,1)S(1)} %shard_map.89), channel_id=1, source_target_pairs={{0,8},{8,0},{16,24},{24,16},{32,40},{40,32},{48,56},{56,48},{64,72... | collective-permute-start | bytes 835592 | tf_op jit(solution)/shard_map/ppermute | solution.py:465
  54.5 28.0 %all-to-all-start.2 = ((bf16[8,256,128]{2,1,0:T(8,128)(2,1)}), bf16[8,256,128]{2,1,0:T(8,128)(2,1)S(1)}, u32[]{:S(2)}, u32[]{:S(2)}) async-start(bf16[8,256,128]{2,1,0:T(8,128)(2,1)} %shard_map.91), calls=%async_computation.2 | async-start | bytes 1048576 | tf_op jit(solution)/shard_map/all_to_all | solution.py:482

commit v5 on v4

--- a/solution.py
+++ b/solution.py
@@ -19,7 +19,8 @@
 PAIRS = 8
 CHUNKS = 8
 ROWS = 16
-SEND_ROWS = 2 * ROWS + 8
+SEND_ROWS = 2 * ROWS + 2
+SEND_TILES = SEND_ROWS // 2
 TAIL = 16
 
 
@@ -90,6 +91,15 @@
 def one_row(rows):
     rows = rows.astype(F32)
     return rows[0:1, :] + rows[1:2, :]
+
+
+def put(ref, k, rows):
+    for j in range(SEND_TILES):
+        ref[k, j] = rows[2 * j : 2 * j + 2]
+
+
+def take(ref, k):
+    return ref[k].reshape(SEND_ROWS, LANES)
 
 
 def load(pairs, sems):
@@ -184,12 +194,11 @@
         chip_opens = factor0 * jnp.where(first, opens, my_opens) + jnp.where(first, my_opens, opens)
         chip_ends = chip_ends.astype(BF16)
         chip_opens = chip_opens.astype(BF16)
-        factors = two_rows(mine * theirs, 8)
+        factors = two_rows(mine * theirs, 2)
         for r in range(CHUNKS):
             rows = slice(r * ROWS, (r + 1) * ROWS)
-            send_ref[i * CHUNKS + r] = jnp.concatenate(
-                [chip_ends[rows], chip_opens[rows], factors], axis=0
-            )
+            block = jnp.concatenate([chip_ends[rows], chip_opens[rows], factors], axis=0)
+            put(send_ref, i * CHUNKS + r, block)
         owners = pl.ds(i * CHUNKS, CHUNKS)
         copies.append(pltpu.make_async_copy(send_ref.at[owners], send_hbm.at[owners], sems.at[i]))
         copies[i].start()
@@ -201,19 +210,17 @@
     count = got_ref.shape[0]
     entry = jnp.zeros((ROWS, LANES), F32)
     adjoint = jnp.zeros((ROWS, LANES), F32)
+    blocks = [take(got_ref, k) for k in range(count)]
     entries, adjoints = [None] * count, [None] * count
     for k in range(count):
         m = count - 1 - k
         entries[k], adjoints[m] = entry, adjoint
-        entry = one_row(got_ref[k, 2 * ROWS : SEND_ROWS]) * entry + got_ref[k, 0:ROWS].astype(F32)
-        adjoint = one_row(got_ref[m, 2 * ROWS : SEND_ROWS]) * adjoint + got_ref[
-            m, ROWS : 2 * ROWS
-        ].astype(F32)
+        entry = one_row(blocks[k][2 * ROWS :]) * entry + blocks[k][0:ROWS].astype(F32)
+        adjoint = one_row(blocks[m][2 * ROWS :]) * adjoint + blocks[m][ROWS : 2 * ROWS].astype(F32)
     for k in range(count):
         overlap = jnp.sum(entries[k] * adjoints[k], axis=0, keepdims=True)
-        back_ref[k] = jnp.concatenate(
-            [entries[k].astype(BF16), adjoints[k].astype(BF16), two_rows(overlap, 8)], axis=0
-        )
+        block = [entries[k].astype(BF16), adjoints[k].astype(BF16), two_rows(overlap, 2)]
+        put(back_ref, k, jnp.concatenate(block, axis=0))
 
 
 def intra_kernel(
@@ -273,18 +280,15 @@
     bc_ref[1] = nn(high_t, b_mat) + nn(low_t, b_mat)
 
 
-def slices(ref, i, start, rows):
-    return ref[i * CHUNKS : (i + 1) * CHUNKS, start : start + rows, :]
-
-
 def block_states(mine, back_ref, got_ref, mine_ref, factor_ref, out_ref):
     inside_is_adjoint = first_core((TOK, LANES)) == mine
     for i in range(PAIRS // 2):
         my_factor = factor_ref[0:1, pair(i)]
         their_factor = one_row(got_ref[2 * TOK : 2 * TOK + TAIL, pair(i)])
-        entry = slices(back_ref, i, 0, ROWS).reshape(TOK, LANES).astype(F32)
-        adjoint = slices(back_ref, i, ROWS, ROWS).reshape(TOK, LANES).astype(F32)
-        chip = one_row(jnp.sum(slices(back_ref, i, 2 * ROWS, 8).astype(F32), axis=0))
+        blocks = [take(back_ref, i * CHUNKS + r) for r in range(CHUNKS)]
+        entry = jnp.concatenate([block[0:ROWS] for block in blocks], axis=0).astype(F32)
+        adjoint = jnp.concatenate([block[ROWS : 2 * ROWS] for block in blocks], axis=0).astype(F32)
+        chip = sum(one_row(block[2 * ROWS :]) for block in blocks)
         if mine:
             opens = got_ref[TOK : 2 * TOK, pair(i)].astype(F32)
             ends = got_ref[0:TOK, pair(i)].astype(F32)
@@ -402,7 +406,7 @@
     wide = (TOK, WIDE)
     half = (TOK, HALF_WIDE)
     states = (2 * TOK + TAIL, HALF_WIDE)
-    slices_shape = (chips, SEND_ROWS, LANES)
+    slices_shape = (chips, SEND_TILES, 2, LANES)
 
     def loaded(shape):
         return (

time: 83.6 us -> 82.1 us (0.982)
  no operation moved by 1% of the time
where the time goes in v5:
time: 82.1 us; the launch traced here: 81.7 us
  starting transfers between devices  28.9 us (35%)
  waiting for transfers between devices  23.5 us (29%)
  blocking collectives  16.7 us (20%)
  Pallas kernels  11.9 us (14%)
    all_to_all x1, blocking collectives, per_device(): lax.all_to_all(back, 'seq', 0, 0, tiled=True, axis_index_groups=same_core)  16.7 us
    all_to_all x1, waiting for transfers between devices, per_device(): parts = lax.all_to_all(parts, 'head', 0, 0, tiled=True)  15.6 us
    pallas_call x10, Pallas kernels, call(): pl.pallas_call(body, out_shape=[jax.ShapeDtypeStruct(s, d) for s, d in ou...  11.9 us
    all_to_all x1, starting transfers between devices, per_device(): parts = lax.all_to_all(parts, 'head', 0, 0, tiled=True)  10 us
    ppermute x1, starting transfers between devices, per_device(): got = lax.ppermute(send, 'seq', swap)  8.79 us
    all_to_all x1, waiting for transfers between devices, per_device(): lax.all_to_all(send, 'seq', 0, 0, tiled=True, axis_index_groups=same_core)  6.58 us
    ppermute x1, starting transfers between devices, per_device(): other = lax.ppermute(send, 'seq', swap)  5.75 us
    all_to_all x1, starting transfers between devices, per_device(): lax.all_to_all(send, 'seq', 0, 0, tiled=True, axis_index_groups=same_core)  4.31 us
  transfers between devices with their start and end apart: 4, of which 4 were waited for; matrix products, arithmetic and copies ran while one was open for 0% of the time, Pallas kernels for 8%

profile of v5, /device:TPU:1, one launch (start us, length us, event | category | flops | bytes accessed | tf_op | source)
XLA Modules:
  0.0 81.7 jit_solution(16056711517563930703)
XLA Ops:
  0.6 1.9 %shard_map.84 = (bf16[272,512]{1,0:T(8,128)(2,1)S(1)}, bf16[128,512]{1,0:T(8,128)(2,1)S(1)}, bf16[128,512]{1,0:T(8,128)(2,1)S(1)}, f32[128,8]{1,0:T(8,128)S(1)},...) custom-call(bf16[128,1024]{1,0:T(8,128)(2,1)} %x_hbm.3, bf16[128,128]{1,0:T(8,128)(2,1)} %b_hbm.3, ...), custom_call_target="tpu_custom_call" | custom-call | flops 1000000000 | bytes 262144 | tf_op jit(solution)/shard_map/pallas_call | solution.py:388
  2.5 8.8 %collective-permute-start = (bf16[272,512]{1,0:T(8,128)(2,1)S(1)}, bf16[272,512]{1,0:T(8,128)(2,1)S(1)}, u32[]{:S(2)}, u32[]{:S(2)}) collective-permute-start(bf16[272,512]{1,0:T(8,128)(2,1)S(1)} %get-tuple-element.36), channel_id=1, source_target_pairs={{0,8},{8,0},{16,24},{24,16},{32,40},{40,32},{48,56},{56,48},{64,72... | collective-permute-start | bytes 835592 | tf_op jit(solution)/shard_map/ppermute | solution.py:430
  11.3 0.6 shard_map.85
  11.9 0.6 collective-permute-done.got_ref
  12.5 0.9 %shard_map.86 = bf16[32,17,2,128]{3,2,1,0:T(2,128)(2,1)} custom-call(bf16[272,512]{1,0:T(8,128)(2,1)S(1)} %collective-permute-done.got_ref, f32[256,512]{1,0:T(8,128)S(1)} %get-tuple-element.42.mine_ref, f32[8,512]{1,0:T(8,128)S(1)} %get-tuple-element.43.factor_ref), custom_call_target="tpu_custom_call" | custom-call | flops 1000000000 | bytes 262144 | tf_op jit(solution)/shard_map/pallas_call | solution.py:388
  13.4 4.3 %all-to-all-start = ((bf16[32,17,2,128]{3,2,1,0:T(2,128)(2,1)}), bf16[32,17,2,128]{3,2,1,0:T(2,128)(2,1)S(1)}, u32[]{:S(2)}, u32[]{:S(2)}) async-start(bf16[32,17,2,128]{3,2,1,0:T(2,128)(2,1)} %shard_map.86), calls=%async_computation | async-start | bytes 557056 | tf_op jit(solution)/shard_map/all_to_all | solution.py:448
  17.7 3.2 %shard_map.87 = (f32[128,1024]{1,0:T(8,128)S(1)}, f32[16,128]{1,0:T(8,128)S(1)}, f32[2,128,128]{2,1,0:T(8,128)S(1)}, bf16[128,1024]{1,0:T(8,128)(2,1)S(1)}, bf16...) custom-call(bf16[128,1024]{1,0:T(8,128)(2,1)} %x_hbm.3, ...), custom_call_target="tpu_custom_call" | custom-call | flops 3000000000 | bytes 262144 | tf_op jit(solution)/shard_map/pallas_call | solution.py:388
  20.9 6.6 %all-to-all-done.got_ref = bf16[32,17,2,128]{3,2,1,0:T(2,128)(2,1)S(1)} async-done(((bf16[32,17,2,128]{3,2,1,0:T(2,128)(2,1)}), bf16[32,17,2,128]{3,2,1,0:T(2,128)(2,1)S(1)}, u32[]{:S(2)}, u32[]{:S(2)}) %all-to-all-start) | async-done | bytes 278560 | tf_op jit(solution)/shard_map/all_to_all | solution.py:448
  27.5 0.4 shard_map.88
  27.9 16.7 %all_to_all.15.back_ref = bf16[32,17,2,128]{3,2,1,0:T(2,128)(2,1)S(1)} all-to-all(bf16[32,17,2,128]{3,2,1,0:T(2,128)(2,1)S(1)} %shard_map.88), channel_id=1, replica_groups={{0,16,32,48,64,80,96,112,128,144,160,176,192,208,224,240,256,272,288,30..., dimensions={0} | all-to-all | bytes 557056 | tf_op jit(solution)/shard_map/all_to_all | solution.py:467
  44.6 0.3 shard_map.89
  44.8 5.8 %collective-permute-start.1 = (bf16[272,512]{1,0:T(8,128)(2,1)S(1)}, bf16[272,512]{1,0:T(8,128)(2,1)S(1)}, u32[]{:S(2)}, u32[]{:S(2)}) collective-permute-start(bf16[272,512]{1,0:T(8,128)(2,1)S(1)} %shard_map.89), channel_id=1, source_target_pairs={{0,8},{8,0},{16,24},{24,16},{32,40},{40,32},{48,56},{56,48},{64,72... | collective-permute-start | bytes 835592 | tf_op jit(solution)/shard_map/ppermute | solution.py:469
  50.6 0.5 shard_map.90
  51.1 0.7 collective-permute-done.1.other_ref
  51.8 1.2 %shard_map.91 = bf16[8,256,128]{2,1,0:T(8,128)(2,1)} custom-call(bf16[272,512]{1,0:T(8,128)(2,1)S(1)} %collective-permute-done.1.other_ref, bf16[128,1024]{1,0:T(8,128)(2,1)S(1)} %get-tuple-element.52.wx_ref, bf16[128,1024]{1,0:T(8,128)(2,1)S(1)} %get-tuple-element.53.wg_ref, f32[2,128,128]{2,1,0:T(8,128)S(1)} %get-tuple-element.55.part_ref), custom_call_target="tpu_custom_call" | custom-call | flops 1000000000 | bytes 262144 | tf_op jit(solution)/shard_map/pallas_call | solution.py:388
  53.0 10.0 %all-to-all-start.2 = ((bf16[8,256,128]{2,1,0:T(8,128)(2,1)}), bf16[8,256,128]{2,1,0:T(8,128)(2,1)S(1)}, u32[]{:S(2)}, u32[]{:S(2)}) async-start(bf16[8,256,128]{2,1,0:T(8,128)(2,1)} %shard_map.91), calls=%async_computation.2 | async-start | bytes 1048576 | tf_op jit(solution)/shard_map/all_to_all | solution.py:486
  63.0 2.3 %shard_map.92 = (bf16[128,1024]{1,0:T(8,128)(2,1)}, f32[16,128]{1,0:T(8,128)}) custom-call(bf16[272,512]{1,0:T(8,128)(2,1)S(1)} %get-tuple-element.56.own_ref, bf16[272,512]{1,0:T(8,128)(2,1)S(1)} %collective-permute-done.1.other_ref, bf16[128,1024]{1,0:T(8,128)(2,1)S(1)} %get-tuple-element.52.wx_ref, bf16[128,1024]{1,0:T(8,128)(2,1)S(1)} %get-tuple-element.53.wg_ref, ...), custom_call_target="tpu_custom_call" | custom-call | flops 3000000000 | bytes 262144 | tf_op jit(solution)/shard_map/pallas_call | solution.py:388
  65.4 15.6 %all-to-all-done.2.parts_ref = bf16[8,256,128]{2,1,0:T(8,128)(2,1)S(1)} async-done(((bf16[8,256,128]{2,1,0:T(8,128)(2,1)}), bf16[8,256,128]{2,1,0:T(8,128)(2,1)S(1)}, u32[]{:S(2)}, u32[]{:S(2)}) %all-to-all-start.2) | async-done | bytes 524320 | tf_op jit(solution)/shard_map/all_to_all | solution.py:486
  81.0 0.7 shard_map.93
Async XLA Ops:
  2.5 10.0 %collective-permute-start = (bf16[272,512]{1,0:T(8,128)(2,1)S(1)}, bf16[272,512]{1,0:T(8,128)(2,1)S(1)}, u32[]{:S(2)}, u32[]{:S(2)}) collective-permute-start(bf16[272,512]{1,0:T(8,128)(2,1)S(1)} %get-tuple-element.36), channel_id=1, source_target_pairs={{0,8},{8,0},{16,24},{24,16},{32,40},{40,32},{48,56},{56,48},{64,72... | collective-permute-start | bytes 835592 | tf_op jit(solution)/shard_map/ppermute | solution.py:430
  13.4 14.1 %all-to-all-start = ((bf16[32,17,2,128]{3,2,1,0:T(2,128)(2,1)}), bf16[32,17,2,128]{3,2,1,0:T(2,128)(2,1)S(1)}, u32[]{:S(2)}, u32[]{:S(2)}) async-start(bf16[32,17,2,128]{3,2,1,0:T(2,128)(2,1)} %shard_map.86), calls=%async_computation | async-start | bytes 557056 | tf_op jit(solution)/shard_map/all_to_all | solution.py:448
  44.8 6.9 %collective-permute-start.1 = (bf16[272,512]{1,0:T(8,128)(2,1)S(1)}, bf16[272,512]{1,0:T(8,128)(2,1)S(1)}, u32[]{:S(2)}, u32[]{:S(2)}) collective-permute-start(bf16[272,512]{1,0:T(8,128)(2,1)S(1)} %shard_map.89), channel_id=1, source_target_pairs={{0,8},{8,0},{16,24},{24,16},{32,40},{40,32},{48,56},{56,48},{64,72... | collective-permute-start | bytes 835592 | tf_op jit(solution)/shard_map/ppermute | solution.py:469
  53.0 28.0 %all-to-all-start.2 = ((bf16[8,256,128]{2,1,0:T(8,128)(2,1)}), bf16[8,256,128]{2,1,0:T(8,128)(2,1)S(1)}, u32[]{:S(2)}, u32[]{:S(2)}) async-start(bf16[8,256,128]{2,1,0:T(8,128)(2,1)} %shard_map.91), calls=%async_computation.2 | async-start | bytes 1048576 | tf_op jit(solution)/shard_map/all_to_all | solution.py:486

commit v6 on v5

--- a/solution.py
+++ b/solution.py
@@ -21,6 +21,7 @@
 ROWS = 16
 SEND_ROWS = 2 * ROWS + 2
 SEND_TILES = SEND_ROWS // 2
+LEAD = 20
 TAIL = 16
 
 
@@ -206,11 +207,12 @@
         copy.wait()
 
 
-def recurrence_kernel(got_ref, back_ref):
+def recurrence_kernel(lead, got_ref, back_ref):
     count = got_ref.shape[0]
     entry = jnp.zeros((ROWS, LANES), F32)
     adjoint = jnp.zeros((ROWS, LANES), F32)
-    blocks = [take(got_ref, k) for k in range(count)]
+    place = [(k - lead) % count for k in range(count)]
+    blocks = [take(got_ref, place[k]) for k in range(count)]
     entries, adjoints = [None] * count, [None] * count
     for k in range(count):
         m = count - 1 - k
@@ -220,7 +222,7 @@
     for k in range(count):
         overlap = jnp.sum(entries[k] * adjoints[k], axis=0, keepdims=True)
         block = [entries[k].astype(BF16), adjoints[k].astype(BF16), two_rows(overlap, 2)]
-        put(back_ref, k, jnp.concatenate(block, axis=0))
+        put(back_ref, place[k], jnp.concatenate(block, axis=0))
 
 
 def intra_kernel(
@@ -402,7 +404,8 @@
     assert chips == PAIRS // 2 * CHUNKS
     inputs = (x, b_mat, c_mat, log_decay, grad)
     swap = [(i, i ^ 1) for i in range(seq)]
-    same_core = [[2 * m + c for m in range(chips)] for c in range(2)]
+    lead = LEAD
+    same_core = [[2 * ((m + lead) % chips) + c for m in range(chips)] for c in range(2)]
     wide = (TOK, WIDE)
     half = (TOK, HALF_WIDE)
     states = (2 * TOK + TAIL, HALF_WIDE)
@@ -463,7 +466,7 @@
         scratch=loaded(wide) + (pltpu.SemaphoreType.DMA((5,)),),
     )
     gathered, (gx, inner, bc, wx, wg, mats, end) = lax.optimization_barrier((gathered, local))
-    (back,) = call(recurrence_kernel, [(slices_shape, BF16)], 1, gathered)
+    (back,) = call(functools.partial(recurrence_kernel, lead), [(slices_shape, BF16)], 1, gathered)
     back = lax.all_to_all(back, "seq", 0, 0, tiled=True, axis_index_groups=same_core)
     (send,) = call(their_block_kernel, [(states, BF16)], 1, back, got, mine, factor)
     other = lax.ppermute(send, "seq", swap)

time: 82.1 us -> 77.9 us (0.949)
  waiting for transfers between devices: 23.5 us -> 20.8 us
  blocking collectives: 16.7 us -> 15.2 us
    all_to_all x1, starting transfers between devices: 4.31 us -> 9.22 us  [per_device(): lax.all_to_all(send, 'seq', 0, 0, tiled=True, axis_index_groups=same_core)]
    all_to_all x1, starting transfers between devices: 10 us -> 7.02 us  [per_device(): parts = lax.all_to_all(parts, 'head', 0, 0, tiled=True)]
    all_to_all x1, waiting for transfers between devices: 6.58 us -> 3.96 us  [per_device(): lax.all_to_all(send, 'seq', 0, 0, tiled=True, axis_index_groups=same_core)]
    ppermute x1, starting transfers between devices: 5.75 us -> 3.75 us  [per_device(): other = lax.ppermute(send, 'seq', swap)]
    all_to_all x1, blocking collectives: 16.7 us -> 15.2 us  [per_device(): lax.all_to_all(back, 'seq', 0, 0, tiled=True, axis_index_groups=same_core)]
where the time goes in v6:
time: 77.9 us; the launch traced here: 77.5 us
  starting transfers between devices  28.8 us (37%)
  waiting for transfers between devices  20.8 us (27%)
  blocking collectives  15.2 us (20%)
  Pallas kernels  11.9 us (15%)
    all_to_all x1, waiting for transfers between devices, per_device(): parts = lax.all_to_all(parts, 'head', 0, 0, tiled=True)  15.6 us
    all_to_all x1, blocking collectives, per_device(): lax.all_to_all(back, 'seq', 0, 0, tiled=True, axis_index_groups=same_core)  15.2 us
    pallas_call x10, Pallas kernels, call(): pl.pallas_call(body, out_shape=[jax.ShapeDtypeStruct(s, d) for s, d in ou...  11.9 us
    all_to_all x1, starting transfers between devices, per_device(): lax.all_to_all(send, 'seq', 0, 0, tiled=True, axis_index_groups=same_core)  9.22 us
    ppermute x1, starting transfers between devices, per_device(): got = lax.ppermute(send, 'seq', swap)  8.79 us
    all_to_all x1, starting transfers between devices, per_device(): parts = lax.all_to_all(parts, 'head', 0, 0, tiled=True)  7.02 us
    all_to_all x1, waiting for transfers between devices, per_device(): lax.all_to_all(send, 'seq', 0, 0, tiled=True, axis_index_groups=same_core)  3.96 us
    ppermute x1, starting transfers between devices, per_device(): other = lax.ppermute(send, 'seq', swap)  3.75 us
  transfers between devices with their start and end apart: 4, of which 4 were waited for; matrix products, arithmetic and copies ran while one was open for 0% of the time, Pallas kernels for 8%

profile of v6, /device:TPU:1, one launch (start us, length us, event | category | flops | bytes accessed | tf_op | source)
XLA Modules:
  0.0 77.5 jit_solution(15527181212524233735)
XLA Ops:
  0.6 1.9 %shard_map.84 = (bf16[272,512]{1,0:T(8,128)(2,1)S(1)}, bf16[128,512]{1,0:T(8,128)(2,1)S(1)}, bf16[128,512]{1,0:T(8,128)(2,1)S(1)}, f32[128,8]{1,0:T(8,128)S(1)},...) custom-call(bf16[128,1024]{1,0:T(8,128)(2,1)} %x_hbm.3, bf16[128,128]{1,0:T(8,128)(2,1)} %b_hbm.3, ...), custom_call_target="tpu_custom_call" | custom-call | flops 1000000000 | bytes 262144 | tf_op jit(solution)/shard_map/pallas_call | solution.py:390
  2.5 8.8 %collective-permute-start = (bf16[272,512]{1,0:T(8,128)(2,1)S(1)}, bf16[272,512]{1,0:T(8,128)(2,1)S(1)}, u32[]{:S(2)}, u32[]{:S(2)}) collective-permute-start(bf16[272,512]{1,0:T(8,128)(2,1)S(1)} %get-tuple-element.36), channel_id=1, source_target_pairs={{0,8},{8,0},{16,24},{24,16},{32,40},{40,32},{48,56},{56,48},{64,72... | collective-permute-start | bytes 835592 | tf_op jit(solution)/shard_map/ppermute | solution.py:433
  11.3 0.6 shard_map.85
  11.9 0.6 collective-permute-done.got_ref
  12.5 0.9 %shard_map.86 = bf16[32,17,2,128]{3,2,1,0:T(2,128)(2,1)} custom-call(bf16[272,512]{1,0:T(8,128)(2,1)S(1)} %collective-permute-done.got_ref, f32[256,512]{1,0:T(8,128)S(1)} %get-tuple-element.42.mine_ref, f32[8,512]{1,0:T(8,128)S(1)} %get-tuple-element.43.factor_ref), custom_call_target="tpu_custom_call" | custom-call | flops 1000000000 | bytes 262144 | tf_op jit(solution)/shard_map/pallas_call | solution.py:390
  13.4 9.2 %all-to-all-start = ((bf16[32,17,2,128]{3,2,1,0:T(2,128)(2,1)}), bf16[32,17,2,128]{3,2,1,0:T(2,128)(2,1)S(1)}, u32[]{:S(2)}, u32[]{:S(2)}) async-start(bf16[32,17,2,128]{3,2,1,0:T(2,128)(2,1)} %shard_map.86), calls=%async_computation | async-start | bytes 557056 | tf_op jit(solution)/shard_map/all_to_all | solution.py:451
  22.6 3.2 %shard_map.87 = (f32[128,1024]{1,0:T(8,128)S(1)}, f32[16,128]{1,0:T(8,128)S(1)}, f32[2,128,128]{2,1,0:T(8,128)S(1)}, bf16[128,1024]{1,0:T(8,128)(2,1)S(1)}, bf16...) custom-call(bf16[128,1024]{1,0:T(8,128)(2,1)} %x_hbm.3, ...), custom_call_target="tpu_custom_call" | custom-call | flops 3000000000 | bytes 262144 | tf_op jit(solution)/shard_map/pallas_call | solution.py:390
  25.8 4.0 %all-to-all-done.got_ref = bf16[32,17,2,128]{3,2,1,0:T(2,128)(2,1)S(1)} async-done(((bf16[32,17,2,128]{3,2,1,0:T(2,128)(2,1)}), bf16[32,17,2,128]{3,2,1,0:T(2,128)(2,1)S(1)}, u32[]{:S(2)}, u32[]{:S(2)}) %all-to-all-start) | async-done | bytes 278560 | tf_op jit(solution)/shard_map/all_to_all | solution.py:451
  29.8 0.4 shard_map.88
  30.2 15.2 %all_to_all.15.back_ref = bf16[32,17,2,128]{3,2,1,0:T(2,128)(2,1)S(1)} all-to-all(bf16[32,17,2,128]{3,2,1,0:T(2,128)(2,1)S(1)} %shard_map.88), channel_id=1, replica_groups={{320,336,352,368,384,400,416,432,448,464,480,496,0,16,32,48,64,80,96,11..., dimensions={0} | all-to-all | bytes 557056 | tf_op jit(solution)/shard_map/all_to_all | solution.py:470
  45.4 0.3 shard_map.89
  45.6 3.7 %collective-permute-start.1 = (bf16[272,512]{1,0:T(8,128)(2,1)S(1)}, bf16[272,512]{1,0:T(8,128)(2,1)S(1)}, u32[]{:S(2)}, u32[]{:S(2)}) collective-permute-start(bf16[272,512]{1,0:T(8,128)(2,1)S(1)} %shard_map.89), channel_id=1, source_target_pairs={{0,8},{8,0},{16,24},{24,16},{32,40},{40,32},{48,56},{56,48},{64,72... | collective-permute-start | bytes 835592 | tf_op jit(solution)/shard_map/ppermute | solution.py:472
  49.4 0.5 shard_map.90
  49.9 0.7 collective-permute-done.1.other_ref
  50.6 1.2 %shard_map.91 = bf16[8,256,128]{2,1,0:T(8,128)(2,1)} custom-call(bf16[272,512]{1,0:T(8,128)(2,1)S(1)} %collective-permute-done.1.other_ref, bf16[128,1024]{1,0:T(8,128)(2,1)S(1)} %get-tuple-element.52.wx_ref, bf16[128,1024]{1,0:T(8,128)(2,1)S(1)} %get-tuple-element.53.wg_ref, f32[2,128,128]{2,1,0:T(8,128)S(1)} %get-tuple-element.55.part_ref), custom_call_target="tpu_custom_call" | custom-call | flops 1000000000 | bytes 262144 | tf_op jit(solution)/shard_map/pallas_call | solution.py:390
  51.8 7.0 %all-to-all-start.2 = ((bf16[8,256,128]{2,1,0:T(8,128)(2,1)}), bf16[8,256,128]{2,1,0:T(8,128)(2,1)S(1)}, u32[]{:S(2)}, u32[]{:S(2)}) async-start(bf16[8,256,128]{2,1,0:T(8,128)(2,1)} %shard_map.91), calls=%async_computation.2 | async-start | bytes 1048576 | tf_op jit(solution)/shard_map/all_to_all | solution.py:489
  58.8 2.3 %shard_map.92 = (bf16[128,1024]{1,0:T(8,128)(2,1)}, f32[16,128]{1,0:T(8,128)}) custom-call(bf16[272,512]{1,0:T(8,128)(2,1)S(1)} %get-tuple-element.56.own_ref, bf16[272,512]{1,0:T(8,128)(2,1)S(1)} %collective-permute-done.1.other_ref, bf16[128,1024]{1,0:T(8,128)(2,1)S(1)} %get-tuple-element.52.wx_ref, bf16[128,1024]{1,0:T(8,128)(2,1)S(1)} %get-tuple-element.53.wg_ref, ...), custom_call_target="tpu_custom_call" | custom-call | flops 3000000000 | bytes 262144 | tf_op jit(solution)/shard_map/pallas_call | solution.py:390
  61.2 15.6 %all-to-all-done.2.parts_ref = bf16[8,256,128]{2,1,0:T(8,128)(2,1)S(1)} async-done(((bf16[8,256,128]{2,1,0:T(8,128)(2,1)}), bf16[8,256,128]{2,1,0:T(8,128)(2,1)S(1)}, u32[]{:S(2)}, u32[]{:S(2)}) %all-to-all-start.2) | async-done | bytes 524320 | tf_op jit(solution)/shard_map/all_to_all | solution.py:489
  76.8 0.7 shard_map.93
Async XLA Ops:
  2.5 10.0 %collective-permute-start = (bf16[272,512]{1,0:T(8,128)(2,1)S(1)}, bf16[272,512]{1,0:T(8,128)(2,1)S(1)}, u32[]{:S(2)}, u32[]{:S(2)}) collective-permute-start(bf16[272,512]{1,0:T(8,128)(2,1)S(1)} %get-tuple-element.36), channel_id=1, source_target_pairs={{0,8},{8,0},{16,24},{24,16},{32,40},{40,32},{48,56},{56,48},{64,72... | collective-permute-start | bytes 835592 | tf_op jit(solution)/shard_map/ppermute | solution.py:433
  13.4 16.4 %all-to-all-start = ((bf16[32,17,2,128]{3,2,1,0:T(2,128)(2,1)}), bf16[32,17,2,128]{3,2,1,0:T(2,128)(2,1)S(1)}, u32[]{:S(2)}, u32[]{:S(2)}) async-start(bf16[32,17,2,128]{3,2,1,0:T(2,128)(2,1)} %shard_map.86), calls=%async_computation | async-start | bytes 557056 | tf_op jit(solution)/shard_map/all_to_all | solution.py:451
  45.6 4.9 %collective-permute-start.1 = (bf16[272,512]{1,0:T(8,128)(2,1)S(1)}, bf16[272,512]{1,0:T(8,128)(2,1)S(1)}, u32[]{:S(2)}, u32[]{:S(2)}) collective-permute-start(bf16[272,512]{1,0:T(8,128)(2,1)S(1)} %shard_map.89), channel_id=1, source_target_pairs={{0,8},{8,0},{16,24},{24,16},{32,40},{40,32},{48,56},{56,48},{64,72... | collective-permute-start | bytes 835592 | tf_op jit(solution)/shard_map/ppermute | solution.py:472
  51.8 25.0 %all-to-all-start.2 = ((bf16[8,256,128]{2,1,0:T(8,128)(2,1)}), bf16[8,256,128]{2,1,0:T(8,128)(2,1)S(1)}, u32[]{:S(2)}, u32[]{:S(2)}) async-start(bf16[8,256,128]{2,1,0:T(8,128)(2,1)} %shard_map.91), calls=%async_computation.2 | async-start | bytes 1048576 | tf_op jit(solution)/shard_map/all_to_all | solution.py:489

commit v7 on v6

--- a/solution.py
+++ b/solution.py
@@ -406,6 +406,7 @@
     swap = [(i, i ^ 1) for i in range(seq)]
     lead = LEAD
     same_core = [[2 * ((m + lead) % chips) + c for m in range(chips)] for c in range(2)]
+    last_plane_first = [[(z + heads - 1) % heads for z in range(heads)]]
     wide = (TOK, WIDE)
     half = (TOK, HALF_WIDE)
     states = (2 * TOK + TAIL, HALF_WIDE)
@@ -486,7 +487,7 @@
         to_hbm=True,
         scratch=(pltpu.VMEM((2 * TOK, LANES), BF16), pltpu.SemaphoreType.DMA((2, heads))),
     )
-    parts = lax.all_to_all(parts, "head", 0, 0, tiled=True)
+    parts = lax.all_to_all(parts, "head", 0, 0, tiled=True, axis_index_groups=last_plane_first)
     grad_x, decay_grad = call(
         grads_kernel,
         [(wide, BF16), ((HEADS, TOK), F32)],

time: 77.9 us -> 75.5 us (0.969)
  waiting for transfers between devices: 20.8 us -> 16.2 us
  starting transfers between devices: 28.8 us -> 30.9 us
    all_to_all x1, waiting for transfers between devices: 15.6 us -> 11 us  [per_device(): lax.all_to_all(parts, 'head', 0, 0, tiled=True, axis_index_groups=last_pl...]
    all_to_all x1, starting transfers between devices: 7.02 us -> 9.14 us  [per_device(): lax.all_to_all(parts, 'head', 0, 0, tiled=True, axis_index_groups=last_pl...]
  transfers between devices with their start and end apart: 4 -> 4, of which waited for: 4 -> 4; matrix products, arithmetic and copies ran while one was open for 0% -> 0% of each run, Pallas kernels for 8% -> 9%
where the time goes in v7:
time: 75.5 us; the launch traced here: 75 us
  starting transfers between devices  30.9 us (41%)
  waiting for transfers between devices  16.2 us (21%)
  blocking collectives  15.2 us (20%)
  Pallas kernels  11.9 us (16%)
    all_to_all x1, blocking collectives, per_device(): lax.all_to_all(back, 'seq', 0, 0, tiled=True, axis_index_groups=same_core)  15.2 us
    pallas_call x10, Pallas kernels, call(): pl.pallas_call(body, out_shape=[jax.ShapeDtypeStruct(s, d) for s, d in ou...  11.9 us
    all_to_all x1, waiting for transfers between devices, per_device(): lax.all_to_all(parts, 'head', 0, 0, tiled=True, axis_index_groups=last_pl...  11 us
    all_to_all x1, starting transfers between devices, per_device(): lax.all_to_all(send, 'seq', 0, 0, tiled=True, axis_index_groups=same_core)  9.22 us
    all_to_all x1, starting transfers between devices, per_device(): lax.all_to_all(parts, 'head', 0, 0, tiled=True, axis_index_groups=last_pl...  9.14 us
    ppermute x1, starting transfers between devices, per_device(): got = lax.ppermute(send, 'seq', swap)  8.79 us
    all_to_all x1, waiting for transfers between devices, per_device(): lax.all_to_all(send, 'seq', 0, 0, tiled=True, axis_index_groups=same_core)  3.96 us
    ppermute x1, starting transfers between devices, per_device(): other = lax.ppermute(send, 'seq', swap)  3.75 us
  transfers between devices with their start and end apart: 4, of which 4 were waited for; matrix products, arithmetic and copies ran while one was open for 0% of the time, Pallas kernels for 9%

profile of v7, /device:TPU:1, one launch (start us, length us, event | category | flops | bytes accessed | tf_op | source)
XLA Modules:
  0.0 75.0 jit_solution(10099322973108249547)
XLA Ops:
  0.6 1.9 %shard_map.84 = (bf16[272,512]{1,0:T(8,128)(2,1)S(1)}, bf16[128,512]{1,0:T(8,128)(2,1)S(1)}, bf16[128,512]{1,0:T(8,128)(2,1)S(1)}, f32[128,8]{1,0:T(8,128)S(1)},...) custom-call(bf16[128,1024]{1,0:T(8,128)(2,1)} %x_hbm.3, bf16[128,128]{1,0:T(8,128)(2,1)} %b_hbm.3, ...), custom_call_target="tpu_custom_call" | custom-call | flops 1000000000 | bytes 262144 | tf_op jit(solution)/shard_map/pallas_call | solution.py:390
  2.5 8.8 %collective-permute-start = (bf16[272,512]{1,0:T(8,128)(2,1)S(1)}, bf16[272,512]{1,0:T(8,128)(2,1)S(1)}, u32[]{:S(2)}, u32[]{:S(2)}) collective-permute-start(bf16[272,512]{1,0:T(8,128)(2,1)S(1)} %get-tuple-element.36), channel_id=1, source_target_pairs={{0,8},{8,0},{16,24},{24,16},{32,40},{40,32},{48,56},{56,48},{64,72... | collective-permute-start | bytes 835592 | tf_op jit(solution)/shard_map/ppermute | solution.py:434
  11.3 0.6 shard_map.85
  11.9 0.6 collective-permute-done.got_ref
  12.5 0.9 %shard_map.86 = bf16[32,17,2,128]{3,2,1,0:T(2,128)(2,1)} custom-call(bf16[272,512]{1,0:T(8,128)(2,1)S(1)} %collective-permute-done.got_ref, f32[256,512]{1,0:T(8,128)S(1)} %get-tuple-element.42.mine_ref, f32[8,512]{1,0:T(8,128)S(1)} %get-tuple-element.43.factor_ref), custom_call_target="tpu_custom_call" | custom-call | flops 1000000000 | bytes 262144 | tf_op jit(solution)/shard_map/pallas_call | solution.py:390
  13.4 9.2 %all-to-all-start = ((bf16[32,17,2,128]{3,2,1,0:T(2,128)(2,1)}), bf16[32,17,2,128]{3,2,1,0:T(2,128)(2,1)S(1)}, u32[]{:S(2)}, u32[]{:S(2)}) async-start(bf16[32,17,2,128]{3,2,1,0:T(2,128)(2,1)} %shard_map.86), calls=%async_computation | async-start | bytes 557056 | tf_op jit(solution)/shard_map/all_to_all | solution.py:452
  22.6 3.2 %shard_map.87 = (f32[128,1024]{1,0:T(8,128)S(1)}, f32[16,128]{1,0:T(8,128)S(1)}, f32[2,128,128]{2,1,0:T(8,128)S(1)}, bf16[128,1024]{1,0:T(8,128)(2,1)S(1)}, bf16...) custom-call(bf16[128,1024]{1,0:T(8,128)(2,1)} %x_hbm.3, ...), custom_call_target="tpu_custom_call" | custom-call | flops 3000000000 | bytes 262144 | tf_op jit(solution)/shard_map/pallas_call | solution.py:390
  25.8 4.0 %all-to-all-done.got_ref = bf16[32,17,2,128]{3,2,1,0:T(2,128)(2,1)S(1)} async-done(((bf16[32,17,2,128]{3,2,1,0:T(2,128)(2,1)}), bf16[32,17,2,128]{3,2,1,0:T(2,128)(2,1)S(1)}, u32[]{:S(2)}, u32[]{:S(2)}) %all-to-all-start) | async-done | bytes 278560 | tf_op jit(solution)/shard_map/all_to_all | solution.py:452
  29.8 0.4 shard_map.88
  30.2 15.2 %all_to_all.15.back_ref = bf16[32,17,2,128]{3,2,1,0:T(2,128)(2,1)S(1)} all-to-all(bf16[32,17,2,128]{3,2,1,0:T(2,128)(2,1)S(1)} %shard_map.88), channel_id=1, replica_groups={{320,336,352,368,384,400,416,432,448,464,480,496,0,16,32,48,64,80,96,11..., dimensions={0} | all-to-all | bytes 557056 | tf_op jit(solution)/shard_map/all_to_all | solution.py:471
  45.4 0.3 shard_map.89
  45.6 3.7 %collective-permute-start.1 = (bf16[272,512]{1,0:T(8,128)(2,1)S(1)}, bf16[272,512]{1,0:T(8,128)(2,1)S(1)}, u32[]{:S(2)}, u32[]{:S(2)}) collective-permute-start(bf16[272,512]{1,0:T(8,128)(2,1)S(1)} %shard_map.89), channel_id=1, source_target_pairs={{0,8},{8,0},{16,24},{24,16},{32,40},{40,32},{48,56},{56,48},{64,72... | collective-permute-start | bytes 835592 | tf_op jit(solution)/shard_map/ppermute | solution.py:473
  49.4 0.5 shard_map.90
  49.9 0.7 collective-permute-done.1.other_ref
  50.6 1.2 %shard_map.91 = bf16[8,256,128]{2,1,0:T(8,128)(2,1)} custom-call(bf16[272,512]{1,0:T(8,128)(2,1)S(1)} %collective-permute-done.1.other_ref, bf16[128,1024]{1,0:T(8,128)(2,1)S(1)} %get-tuple-element.52.wx_ref, bf16[128,1024]{1,0:T(8,128)(2,1)S(1)} %get-tuple-element.53.wg_ref, f32[2,128,128]{2,1,0:T(8,128)S(1)} %get-tuple-element.55.part_ref), custom_call_target="tpu_custom_call" | custom-call | flops 1000000000 | bytes 262144 | tf_op jit(solution)/shard_map/pallas_call | solution.py:390
  51.8 9.1 %all-to-all-start.2 = ((bf16[8,256,128]{2,1,0:T(8,128)(2,1)}), bf16[8,256,128]{2,1,0:T(8,128)(2,1)S(1)}, u32[]{:S(2)}, u32[]{:S(2)}) async-start(bf16[8,256,128]{2,1,0:T(8,128)(2,1)} %shard_map.91), calls=%async_computation.2 | async-start | bytes 1048576 | tf_op jit(solution)/shard_map/all_to_all | solution.py:490
  61.0 2.3 %shard_map.92 = (bf16[128,1024]{1,0:T(8,128)(2,1)}, f32[16,128]{1,0:T(8,128)}) custom-call(bf16[272,512]{1,0:T(8,128)(2,1)S(1)} %get-tuple-element.56.own_ref, bf16[272,512]{1,0:T(8,128)(2,1)S(1)} %collective-permute-done.1.other_ref, bf16[128,1024]{1,0:T(8,128)(2,1)S(1)} %get-tuple-element.52.wx_ref, bf16[128,1024]{1,0:T(8,128)(2,1)S(1)} %get-tuple-element.53.wg_ref, ...), custom_call_target="tpu_custom_call" | custom-call | flops 3000000000 | bytes 262144 | tf_op jit(solution)/shard_map/pallas_call | solution.py:390
  63.3 11.0 %all-to-all-done.2.parts_ref = bf16[8,256,128]{2,1,0:T(8,128)(2,1)S(1)} async-done(((bf16[8,256,128]{2,1,0:T(8,128)(2,1)}), bf16[8,256,128]{2,1,0:T(8,128)(2,1)S(1)}, u32[]{:S(2)}, u32[]{:S(2)}) %all-to-all-start.2) | async-done | bytes 524320 | tf_op jit(solution)/shard_map/all_to_all | solution.py:490
  74.3 0.7 shard_map.93
Async XLA Ops:
  2.5 10.0 %collective-permute-start = (bf16[272,512]{1,0:T(8,128)(2,1)S(1)}, bf16[272,512]{1,0:T(8,128)(2,1)S(1)}, u32[]{:S(2)}, u32[]{:S(2)}) collective-permute-start(bf16[272,512]{1,0:T(8,128)(2,1)S(1)} %get-tuple-element.36), channel_id=1, source_target_pairs={{0,8},{8,0},{16,24},{24,16},{32,40},{40,32},{48,56},{56,48},{64,72... | collective-permute-start | bytes 835592 | tf_op jit(solution)/shard_map/ppermute | solution.py:434
  13.4 16.4 %all-to-all-start = ((bf16[32,17,2,128]{3,2,1,0:T(2,128)(2,1)}), bf16[32,17,2,128]{3,2,1,0:T(2,128)(2,1)S(1)}, u32[]{:S(2)}, u32[]{:S(2)}) async-start(bf16[32,17,2,128]{3,2,1,0:T(2,128)(2,1)} %shard_map.86), calls=%async_computation | async-start | bytes 557056 | tf_op jit(solution)/shard_map/all_to_all | solution.py:452
  45.6 4.9 %collective-permute-start.1 = (bf16[272,512]{1,0:T(8,128)(2,1)S(1)}, bf16[272,512]{1,0:T(8,128)(2,1)S(1)}, u32[]{:S(2)}, u32[]{:S(2)}) collective-permute-start(bf16[272,512]{1,0:T(8,128)(2,1)S(1)} %shard_map.89), channel_id=1, source_target_pairs={{0,8},{8,0},{16,24},{24,16},{32,40},{40,32},{48,56},{56,48},{64,72... | collective-permute-start | bytes 835592 | tf_op jit(solution)/shard_map/ppermute | solution.py:473
  51.8 22.5 %all-to-all-start.2 = ((bf16[8,256,128]{2,1,0:T(8,128)(2,1)}), bf16[8,256,128]{2,1,0:T(8,128)(2,1)S(1)}, u32[]{:S(2)}, u32[]{:S(2)}) async-start(bf16[8,256,128]{2,1,0:T(8,128)(2,1)} %shard_map.91), calls=%async_computation.2 | async-start | bytes 1048576 | tf_op jit(solution)/shard_map/all_to_all | solution.py:490

commit v8 on v6

--- a/solution.py
+++ b/solution.py
@@ -21,7 +21,9 @@
 ROWS = 16
 SEND_ROWS = 2 * ROWS + 2
 SEND_TILES = SEND_ROWS // 2
-LEAD = 20
+LAST_CHIP = 20
+CHIP_STRIDE = 11
+PLANE_STRIDE = 3
 TAIL = 16
 
 
@@ -207,11 +209,10 @@
         copy.wait()
 
 
-def recurrence_kernel(lead, got_ref, back_ref):
+def recurrence_kernel(place, got_ref, back_ref):
     count = got_ref.shape[0]
     entry = jnp.zeros((ROWS, LANES), F32)
     adjoint = jnp.zeros((ROWS, LANES), F32)
-    place = [(k - lead) % count for k in range(count)]
     blocks = [take(got_ref, place[k]) for k in range(count)]
     entries, adjoints = [None] * count, [None] * count
     for k in range(count):
@@ -404,8 +405,10 @@
     assert chips == PAIRS // 2 * CHUNKS
     inputs = (x, b_mat, c_mat, log_decay, grad)
     swap = [(i, i ^ 1) for i in range(seq)]
-    lead = LEAD
-    same_core = [[2 * ((m + lead) % chips) + c for m in range(chips)] for c in range(2)]
+    order = [(LAST_CHIP + CHIP_STRIDE * i) % chips for i in range(chips)]
+    place = [order.index(m) for m in range(chips)]
+    same_core = [[2 * m + c for m in order] for c in range(2)]
+    planes = [[(heads - 1 + PLANE_STRIDE * i) % heads for i in range(heads)]]
     wide = (TOK, WIDE)
     half = (TOK, HALF_WIDE)
     states = (2 * TOK + TAIL, HALF_WIDE)
@@ -466,7 +469,7 @@
         scratch=loaded(wide) + (pltpu.SemaphoreType.DMA((5,)),),
     )
     gathered, (gx, inner, bc, wx, wg, mats, end) = lax.optimization_barrier((gathered, local))
-    (back,) = call(functools.partial(recurrence_kernel, lead), [(slices_shape, BF16)], 1, gathered)
+    (back,) = call(functools.partial(recurrence_kernel, place), [(slices_shape, BF16)], 1, gathered)
     back = lax.all_to_all(back, "seq", 0, 0, tiled=True, axis_index_groups=same_core)
     (send,) = call(their_block_kernel, [(states, BF16)], 1, back, got, mine, factor)
     other = lax.ppermute(send, "seq", swap)
@@ -486,7 +489,7 @@
         to_hbm=True,
         scratch=(pltpu.VMEM((2 * TOK, LANES), BF16), pltpu.SemaphoreType.DMA((2, heads))),
     )
-    parts = lax.all_to_all(parts, "head", 0, 0, tiled=True)
+    parts = lax.all_to_all(parts, "head", 0, 0, tiled=True, axis_index_groups=planes)
     grad_x, decay_grad = call(
         grads_kernel,
         [(wide, BF16), ((HEADS, TOK), F32)],

time: 77.9 us -> 75.1 us (0.964)
  the two profiles are of different devices: /device:TPU:1 before, /device:TPU:67 now
where the time goes in v8:
time: 75.1 us; the launch traced here: 74.6 us
  starting transfers between devices  28.6 us (38%)
  waiting for transfers between devices  18.5 us (25%)
  blocking collectives  14.9 us (20%)
  Pallas kernels  11.9 us (16%)
    all_to_all x1, blocking collectives, per_device(): lax.all_to_all(back, 'seq', 0, 0, tiled=True, axis_index_groups=same_core)  14.9 us
    all_to_all x1, waiting for transfers between devices, per_device(): lax.all_to_all(parts, 'head', 0, 0, tiled=True, axis_index_groups=planes)  12.1 us
    pallas_call x10, Pallas kernels, call(): pl.pallas_call(body, out_shape=[jax.ShapeDtypeStruct(s, d) for s, d in ou...  11.9 us
    all_to_all x1, starting transfers between devices, per_device(): lax.all_to_all(parts, 'head', 0, 0, tiled=True, axis_index_groups=planes)  11.3 us
    all_to_all x1, starting transfers between devices, per_device(): lax.all_to_all(send, 'seq', 0, 0, tiled=True, axis_index_groups=same_core)  10.2 us
    all_to_all x1, waiting for transfers between devices, per_device(): lax.all_to_all(send, 'seq', 0, 0, tiled=True, axis_index_groups=same_core)  5.18 us
    ppermute x1, starting transfers between devices, per_device(): other = lax.ppermute(send, 'seq', swap)  4.51 us
    ppermute x1, starting transfers between devices, per_device(): got = lax.ppermute(send, 'seq', swap)  2.59 us
  transfers between devices with their start and end apart: 4, of which 4 were waited for; matrix products, arithmetic and copies ran while one was open for 0% of the time, Pallas kernels for 9%

profile of v8, /device:TPU:67, one launch (start us, length us, event | category | flops | bytes accessed | tf_op | source)
XLA Modules:
  0.0 74.6 jit_solution(7527493827083624342)
XLA Ops:
  0.6 1.9 %shard_map.84 = (bf16[272,512]{1,0:T(8,128)(2,1)S(1)}, bf16[128,512]{1,0:T(8,128)(2,1)S(1)}, bf16[128,512]{1,0:T(8,128)(2,1)S(1)}, f32[128,8]{1,0:T(8,128)S(1)},...) custom-call(bf16[128,1024]{1,0:T(8,128)(2,1)} %x_hbm.3, bf16[128,128]{1,0:T(8,128)(2,1)} %b_hbm.3, ...), custom_call_target="tpu_custom_call" | custom-call | flops 1000000000 | bytes 262144 | tf_op jit(solution)/shard_map/pallas_call | solution.py:391
  2.5 2.6 %collective-permute-start = (bf16[272,512]{1,0:T(8,128)(2,1)S(1)}, bf16[272,512]{1,0:T(8,128)(2,1)S(1)}, u32[]{:S(2)}, u32[]{:S(2)}) collective-permute-start(bf16[272,512]{1,0:T(8,128)(2,1)S(1)} %get-tuple-element.36), channel_id=1, source_target_pairs={{0,8},{8,0},{16,24},{24,16},{32,40},{40,32},{48,56},{56,48},{64,72... | collective-permute-start | bytes 835592 | tf_op jit(solution)/shard_map/ppermute | solution.py:436
  5.1 0.6 shard_map.85
  5.7 0.6 collective-permute-done.got_ref
  6.3 0.9 %shard_map.86 = bf16[32,17,2,128]{3,2,1,0:T(2,128)(2,1)} custom-call(bf16[272,512]{1,0:T(8,128)(2,1)S(1)} %collective-permute-done.got_ref, f32[256,512]{1,0:T(8,128)S(1)} %get-tuple-element.42.mine_ref, f32[8,512]{1,0:T(8,128)S(1)} %get-tuple-element.43.factor_ref), custom_call_target="tpu_custom_call" | custom-call | flops 1000000000 | bytes 262144 | tf_op jit(solution)/shard_map/pallas_call | solution.py:391
  7.2 10.2 %all-to-all-start = ((bf16[32,17,2,128]{3,2,1,0:T(2,128)(2,1)}), bf16[32,17,2,128]{3,2,1,0:T(2,128)(2,1)S(1)}, u32[]{:S(2)}, u32[]{:S(2)}) async-start(bf16[32,17,2,128]{3,2,1,0:T(2,128)(2,1)} %shard_map.86), calls=%async_computation | async-start | bytes 557056 | tf_op jit(solution)/shard_map/all_to_all | solution.py:454
  17.4 3.2 %shard_map.87 = (f32[128,1024]{1,0:T(8,128)S(1)}, f32[16,128]{1,0:T(8,128)S(1)}, f32[2,128,128]{2,1,0:T(8,128)S(1)}, bf16[128,1024]{1,0:T(8,128)(2,1)S(1)}, bf16...) custom-call(bf16[128,1024]{1,0:T(8,128)(2,1)} %x_hbm.3, ...), custom_call_target="tpu_custom_call" | custom-call | flops 3000000000 | bytes 262144 | tf_op jit(solution)/shard_map/pallas_call | solution.py:391
  20.6 5.2 %all-to-all-done.got_ref = bf16[32,17,2,128]{3,2,1,0:T(2,128)(2,1)S(1)} async-done(((bf16[32,17,2,128]{3,2,1,0:T(2,128)(2,1)}), bf16[32,17,2,128]{3,2,1,0:T(2,128)(2,1)S(1)}, u32[]{:S(2)}, u32[]{:S(2)}) %all-to-all-start) | async-done | bytes 278560 | tf_op jit(solution)/shard_map/all_to_all | solution.py:454
  25.7 0.4 shard_map.88
  26.2 14.9 %all_to_all.15.back_ref = bf16[32,17,2,128]{3,2,1,0:T(2,128)(2,1)S(1)} all-to-all(bf16[32,17,2,128]{3,2,1,0:T(2,128)(2,1)S(1)} %shard_map.88), channel_id=1, replica_groups={{320,496,160,336,0,176,352,16,192,368,32,208,384,48,224,400,64,240,416,..., dimensions={0} | all-to-all | bytes 557056 | tf_op jit(solution)/shard_map/all_to_all | solution.py:473
  41.0 0.3 shard_map.89
  41.3 4.5 %collective-permute-start.1 = (bf16[272,512]{1,0:T(8,128)(2,1)S(1)}, bf16[272,512]{1,0:T(8,128)(2,1)S(1)}, u32[]{:S(2)}, u32[]{:S(2)}) collective-permute-start(bf16[272,512]{1,0:T(8,128)(2,1)S(1)} %shard_map.89), channel_id=1, source_target_pairs={{0,8},{8,0},{16,24},{24,16},{32,40},{40,32},{48,56},{56,48},{64,72... | collective-permute-start | bytes 835592 | tf_op jit(solution)/shard_map/ppermute | solution.py:475
  45.8 0.5 shard_map.90
  46.3 0.7 collective-permute-done.1.other_ref
  47.0 1.2 %shard_map.91 = bf16[8,256,128]{2,1,0:T(8,128)(2,1)} custom-call(bf16[272,512]{1,0:T(8,128)(2,1)S(1)} %collective-permute-done.1.other_ref, bf16[128,1024]{1,0:T(8,128)(2,1)S(1)} %get-tuple-element.52.wx_ref, bf16[128,1024]{1,0:T(8,128)(2,1)S(1)} %get-tuple-element.53.wg_ref, f32[2,128,128]{2,1,0:T(8,128)S(1)} %get-tuple-element.55.part_ref), custom_call_target="tpu_custom_call" | custom-call | flops 1000000000 | bytes 262144 | tf_op jit(solution)/shard_map/pallas_call | solution.py:391
  48.2 11.3 %all-to-all-start.2 = ((bf16[8,256,128]{2,1,0:T(8,128)(2,1)}), bf16[8,256,128]{2,1,0:T(8,128)(2,1)S(1)}, u32[]{:S(2)}, u32[]{:S(2)}) async-start(bf16[8,256,128]{2,1,0:T(8,128)(2,1)} %shard_map.91), calls=%async_computation.2 | async-start | bytes 1048576 | tf_op jit(solution)/shard_map/all_to_all | solution.py:492
  59.5 2.3 %shard_map.92 = (bf16[128,1024]{1,0:T(8,128)(2,1)}, f32[16,128]{1,0:T(8,128)}) custom-call(bf16[272,512]{1,0:T(8,128)(2,1)S(1)} %get-tuple-element.56.own_ref, bf16[272,512]{1,0:T(8,128)(2,1)S(1)} %collective-permute-done.1.other_ref, bf16[128,1024]{1,0:T(8,128)(2,1)S(1)} %get-tuple-element.52.wx_ref, bf16[128,1024]{1,0:T(8,128)(2,1)S(1)} %get-tuple-element.53.wg_ref, ...), custom_call_target="tpu_custom_call" | custom-call | flops 3000000000 | bytes 262144 | tf_op jit(solution)/shard_map/pallas_call | solution.py:391
  61.9 12.1 %all-to-all-done.2.parts_ref = bf16[8,256,128]{2,1,0:T(8,128)(2,1)S(1)} async-done(((bf16[8,256,128]{2,1,0:T(8,128)(2,1)}), bf16[8,256,128]{2,1,0:T(8,128)(2,1)S(1)}, u32[]{:S(2)}, u32[]{:S(2)}) %all-to-all-start.2) | async-done | bytes 524320 | tf_op jit(solution)/shard_map/all_to_all | solution.py:492
  74.0 0.7 shard_map.93
Async XLA Ops:
  2.5 3.8 %collective-permute-start = (bf16[272,512]{1,0:T(8,128)(2,1)S(1)}, bf16[272,512]{1,0:T(8,128)(2,1)S(1)}, u32[]{:S(2)}, u32[]{:S(2)}) collective-permute-start(bf16[272,512]{1,0:T(8,128)(2,1)S(1)} %get-tuple-element.36), channel_id=1, source_target_pairs={{0,8},{8,0},{16,24},{24,16},{32,40},{40,32},{48,56},{56,48},{64,72... | collective-permute-start | bytes 835592 | tf_op jit(solution)/shard_map/ppermute | solution.py:436
  7.2 18.5 %all-to-all-start = ((bf16[32,17,2,128]{3,2,1,0:T(2,128)(2,1)}), bf16[32,17,2,128]{3,2,1,0:T(2,128)(2,1)S(1)}, u32[]{:S(2)}, u32[]{:S(2)}) async-start(bf16[32,17,2,128]{3,2,1,0:T(2,128)(2,1)} %shard_map.86), calls=%async_computation | async-start | bytes 557056 | tf_op jit(solution)/shard_map/all_to_all | solution.py:454
  41.3 5.7 %collective-permute-start.1 = (bf16[272,512]{1,0:T(8,128)(2,1)S(1)}, bf16[272,512]{1,0:T(8,128)(2,1)S(1)}, u32[]{:S(2)}, u32[]{:S(2)}) collective-permute-start(bf16[272,512]{1,0:T(8,128)(2,1)S(1)} %shard_map.89), channel_id=1, source_target_pairs={{0,8},{8,0},{16,24},{24,16},{32,40},{40,32},{48,56},{56,48},{64,72... | collective-permute-start | bytes 835592 | tf_op jit(solution)/shard_map/ppermute | solution.py:475
  48.2 25.7 %all-to-all-start.2 = ((bf16[8,256,128]{2,1,0:T(8,128)(2,1)}), bf16[8,256,128]{2,1,0:T(8,128)(2,1)S(1)}, u32[]{:S(2)}, u32[]{:S(2)}) async-start(bf16[8,256,128]{2,1,0:T(8,128)(2,1)} %shard_map.91), calls=%async_computation.2 | async-start | bytes 1048576 | tf_op jit(solution)/shard_map/all_to_all | solution.py:492

commit v9 on v8

--- a/solution.py
+++ b/solution.py
@@ -21,9 +21,8 @@
 ROWS = 16
 SEND_ROWS = 2 * ROWS + 2
 SEND_TILES = SEND_ROWS // 2
-LAST_CHIP = 20
-CHIP_STRIDE = 11
-PLANE_STRIDE = 3
+FIRST_CHIP = 20
+FIRST_PLANE = 5
 TAIL = 16
 
 
@@ -405,10 +404,10 @@
     assert chips == PAIRS // 2 * CHUNKS
     inputs = (x, b_mat, c_mat, log_decay, grad)
     swap = [(i, i ^ 1) for i in range(seq)]
-    order = [(LAST_CHIP + CHIP_STRIDE * i) % chips for i in range(chips)]
+    order = [(FIRST_CHIP + i) % chips for i in range(chips)]
     place = [order.index(m) for m in range(chips)]
     same_core = [[2 * m + c for m in order] for c in range(2)]
-    planes = [[(heads - 1 + PLANE_STRIDE * i) % heads for i in range(heads)]]
+    planes = [[(FIRST_PLANE - i) % heads for i in range(heads)]]
     wide = (TOK, WIDE)
     half = (TOK, HALF_WIDE)
     states = (2 * TOK + TAIL, HALF_WIDE)

time: 75.1 us -> 73.4 us (0.977)
  the two profiles are of different devices: /device:TPU:67 before, /device:TPU:1 now
where the time goes in v9:
time: 73.4 us; the launch traced here: 72.6 us
  starting transfers between devices  30.9 us (42%)
  blocking collectives  15.2 us (21%)
  waiting for transfers between devices  13.8 us (19%)
  Pallas kernels  12 us (16%)
    all_to_all x1, blocking collectives, per_device(): lax.all_to_all(back, 'seq', 0, 0, tiled=True, axis_index_groups=same_core)  15.2 us
    pallas_call x10, Pallas kernels, call(): pl.pallas_call(body, out_shape=[jax.ShapeDtypeStruct(s, d) for s, d in ou...  12 us
    all_to_all x1, starting transfers between devices, per_device(): lax.all_to_all(send, 'seq', 0, 0, tiled=True, axis_index_groups=same_core)  9.22 us
    all_to_all x1, starting transfers between devices, per_device(): lax.all_to_all(parts, 'head', 0, 0, tiled=True, axis_index_groups=planes)  9.15 us
    ppermute x1, starting transfers between devices, per_device(): got = lax.ppermute(send, 'seq', swap)  8.79 us
    all_to_all x1, waiting for transfers between devices, per_device(): lax.all_to_all(parts, 'head', 0, 0, tiled=True, axis_index_groups=planes)  8.6 us
    all_to_all x1, waiting for transfers between devices, per_device(): lax.all_to_all(send, 'seq', 0, 0, tiled=True, axis_index_groups=same_core)  3.96 us
    ppermute x1, starting transfers between devices, per_device(): other = lax.ppermute(send, 'seq', swap)  3.75 us
  transfers between devices with their start and end apart: 4, of which 4 were waited for; matrix products, arithmetic and copies ran while one was open for 0% of the time, Pallas kernels for 9%

profile of v9, /device:TPU:1, one launch (start us, length us, event | category | flops | bytes accessed | tf_op | source)
XLA Modules:
  0.0 72.6 jit_solution(11195450376691624474)
XLA Ops:
  0.6 1.9 %shard_map.84 = (bf16[272,512]{1,0:T(8,128)(2,1)S(1)}, bf16[128,512]{1,0:T(8,128)(2,1)S(1)}, bf16[128,512]{1,0:T(8,128)(2,1)S(1)}, f32[128,8]{1,0:T(8,128)S(1)},...) custom-call(bf16[128,1024]{1,0:T(8,128)(2,1)} %x_hbm.3, bf16[128,128]{1,0:T(8,128)(2,1)} %b_hbm.3, ...), custom_call_target="tpu_custom_call" | custom-call | flops 1000000000 | bytes 262144 | tf_op jit(solution)/shard_map/pallas_call | solution.py:390
  2.5 8.8 %collective-permute-start = (bf16[272,512]{1,0:T(8,128)(2,1)S(1)}, bf16[272,512]{1,0:T(8,128)(2,1)S(1)}, u32[]{:S(2)}, u32[]{:S(2)}) collective-permute-start(bf16[272,512]{1,0:T(8,128)(2,1)S(1)} %get-tuple-element.36), channel_id=1, source_target_pairs={{0,8},{8,0},{16,24},{24,16},{32,40},{40,32},{48,56},{56,48},{64,72... | collective-permute-start | bytes 835592 | tf_op jit(solution)/shard_map/ppermute | solution.py:435
  11.3 0.6 shard_map.85
  11.9 0.6 collective-permute-done.got_ref
  12.5 0.9 %shard_map.86 = bf16[32,17,2,128]{3,2,1,0:T(2,128)(2,1)} custom-call(bf16[272,512]{1,0:T(8,128)(2,1)S(1)} %collective-permute-done.got_ref, f32[256,512]{1,0:T(8,128)S(1)} %get-tuple-element.42.mine_ref, f32[8,512]{1,0:T(8,128)S(1)} %get-tuple-element.43.factor_ref), custom_call_target="tpu_custom_call" | custom-call | flops 1000000000 | bytes 262144 | tf_op jit(solution)/shard_map/pallas_call | solution.py:390
  13.4 9.2 %all-to-all-start = ((bf16[32,17,2,128]{3,2,1,0:T(2,128)(2,1)}), bf16[32,17,2,128]{3,2,1,0:T(2,128)(2,1)S(1)}, u32[]{:S(2)}, u32[]{:S(2)}) async-start(bf16[32,17,2,128]{3,2,1,0:T(2,128)(2,1)} %shard_map.86), calls=%async_computation | async-start | bytes 557056 | tf_op jit(solution)/shard_map/all_to_all | solution.py:453
  22.6 3.2 %shard_map.87 = (f32[128,1024]{1,0:T(8,128)S(1)}, f32[16,128]{1,0:T(8,128)S(1)}, f32[2,128,128]{2,1,0:T(8,128)S(1)}, bf16[128,1024]{1,0:T(8,128)(2,1)S(1)}, bf16...) custom-call(bf16[128,1024]{1,0:T(8,128)(2,1)} %x_hbm.3, ...), custom_call_target="tpu_custom_call" | custom-call | flops 3000000000 | bytes 262144 | tf_op jit(solution)/shard_map/pallas_call | solution.py:390
  25.8 4.0 %all-to-all-done.got_ref = bf16[32,17,2,128]{3,2,1,0:T(2,128)(2,1)S(1)} async-done(((bf16[32,17,2,128]{3,2,1,0:T(2,128)(2,1)}), bf16[32,17,2,128]{3,2,1,0:T(2,128)(2,1)S(1)}, u32[]{:S(2)}, u32[]{:S(2)}) %all-to-all-start) | async-done | bytes 278560 | tf_op jit(solution)/shard_map/all_to_all | solution.py:453
  29.8 0.4 shard_map.88
  30.2 15.2 %all_to_all.15.back_ref = bf16[32,17,2,128]{3,2,1,0:T(2,128)(2,1)S(1)} all-to-all(bf16[32,17,2,128]{3,2,1,0:T(2,128)(2,1)S(1)} %shard_map.88), channel_id=1, replica_groups={{320,336,352,368,384,400,416,432,448,464,480,496,0,16,32,48,64,80,96,11..., dimensions={0} | all-to-all | bytes 557056 | tf_op jit(solution)/shard_map/all_to_all | solution.py:472
  45.4 0.3 shard_map.89
  45.6 3.7 %collective-permute-start.1 = (bf16[272,512]{1,0:T(8,128)(2,1)S(1)}, bf16[272,512]{1,0:T(8,128)(2,1)S(1)}, u32[]{:S(2)}, u32[]{:S(2)}) collective-permute-start(bf16[272,512]{1,0:T(8,128)(2,1)S(1)} %shard_map.89), channel_id=1, source_target_pairs={{0,8},{8,0},{16,24},{24,16},{32,40},{40,32},{48,56},{56,48},{64,72... | collective-permute-start | bytes 835592 | tf_op jit(solution)/shard_map/ppermute | solution.py:474
  49.4 0.5 shard_map.90
  49.9 0.7 collective-permute-done.1.other_ref
  50.6 1.2 %shard_map.91 = bf16[8,256,128]{2,1,0:T(8,128)(2,1)} custom-call(bf16[272,512]{1,0:T(8,128)(2,1)S(1)} %collective-permute-done.1.other_ref, bf16[128,1024]{1,0:T(8,128)(2,1)S(1)} %get-tuple-element.52.wx_ref, bf16[128,1024]{1,0:T(8,128)(2,1)S(1)} %get-tuple-element.53.wg_ref, f32[2,128,128]{2,1,0:T(8,128)S(1)} %get-tuple-element.55.part_ref), custom_call_target="tpu_custom_call" | custom-call | flops 1000000000 | bytes 262144 | tf_op jit(solution)/shard_map/pallas_call | solution.py:390
  51.8 9.1 %all-to-all-start.2 = ((bf16[8,256,128]{2,1,0:T(8,128)(2,1)}), bf16[8,256,128]{2,1,0:T(8,128)(2,1)S(1)}, u32[]{:S(2)}, u32[]{:S(2)}) async-start(bf16[8,256,128]{2,1,0:T(8,128)(2,1)} %shard_map.91), calls=%async_computation.2 | async-start | bytes 1048576 | tf_op jit(solution)/shard_map/all_to_all | solution.py:491
  61.0 2.3 %shard_map.92 = (bf16[128,1024]{1,0:T(8,128)(2,1)}, f32[16,128]{1,0:T(8,128)}) custom-call(bf16[272,512]{1,0:T(8,128)(2,1)S(1)} %get-tuple-element.56.own_ref, bf16[272,512]{1,0:T(8,128)(2,1)S(1)} %collective-permute-done.1.other_ref, bf16[128,1024]{1,0:T(8,128)(2,1)S(1)} %get-tuple-element.52.wx_ref, bf16[128,1024]{1,0:T(8,128)(2,1)S(1)} %get-tuple-element.53.wg_ref, ...), custom_call_target="tpu_custom_call" | custom-call | flops 3000000000 | bytes 262144 | tf_op jit(solution)/shard_map/pallas_call | solution.py:390
  63.3 8.6 %all-to-all-done.2.parts_ref = bf16[8,256,128]{2,1,0:T(8,128)(2,1)S(1)} async-done(((bf16[8,256,128]{2,1,0:T(8,128)(2,1)}), bf16[8,256,128]{2,1,0:T(8,128)(2,1)S(1)}, u32[]{:S(2)}, u32[]{:S(2)}) %all-to-all-start.2) | async-done | bytes 524320 | tf_op jit(solution)/shard_map/all_to_all | solution.py:491
  71.9 0.7 shard_map.93
Async XLA Ops:
  2.5 10.0 %collective-permute-start = (bf16[272,512]{1,0:T(8,128)(2,1)S(1)}, bf16[272,512]{1,0:T(8,128)(2,1)S(1)}, u32[]{:S(2)}, u32[]{:S(2)}) collective-permute-start(bf16[272,512]{1,0:T(8,128)(2,1)S(1)} %get-tuple-element.36), channel_id=1, source_target_pairs={{0,8},{8,0},{16,24},{24,16},{32,40},{40,32},{48,56},{56,48},{64,72... | collective-permute-start | bytes 835592 | tf_op jit(solution)/shard_map/ppermute | solution.py:435
  13.4 16.4 %all-to-all-start = ((bf16[32,17,2,128]{3,2,1,0:T(2,128)(2,1)}), bf16[32,17,2,128]{3,2,1,0:T(2,128)(2,1)S(1)}, u32[]{:S(2)}, u32[]{:S(2)}) async-start(bf16[32,17,2,128]{3,2,1,0:T(2,128)(2,1)} %shard_map.86), calls=%async_computation | async-start | bytes 557056 | tf_op jit(solution)/shard_map/all_to_all | solution.py:453
  45.6 4.9 %collective-permute-start.1 = (bf16[272,512]{1,0:T(8,128)(2,1)S(1)}, bf16[272,512]{1,0:T(8,128)(2,1)S(1)}, u32[]{:S(2)}, u32[]{:S(2)}) collective-permute-start(bf16[272,512]{1,0:T(8,128)(2,1)S(1)} %shard_map.89), channel_id=1, source_target_pairs={{0,8},{8,0},{16,24},{24,16},{32,40},{40,32},{48,56},{56,48},{64,72... | collective-permute-start | bytes 835592 | tf_op jit(solution)/shard_map/ppermute | solution.py:474
  51.8 20.1 %all-to-all-start.2 = ((bf16[8,256,128]{2,1,0:T(8,128)(2,1)}), bf16[8,256,128]{2,1,0:T(8,128)(2,1)S(1)}, u32[]{:S(2)}, u32[]{:S(2)}) async-start(bf16[8,256,128]{2,1,0:T(8,128)(2,1)} %shard_map.91), calls=%async_computation.2 | async-start | bytes 1048576 | tf_op jit(solution)/shard_map/all_to_all | solution.py:491
